TPU v7x, 256 devices: a whole 4x4x8 slice. The times are simulated.
256 devices in a mesh: xy: 8 (over y, x_lo), zt: 32 (over z, x_hi, core).
Axes of the slice: x: 4 (x_hi: 2, x_lo: 2; x = x_hi * 2 + x_lo), y: 4, z: 8, core: 2. Of those that a mesh axis runs over, the one named last changes fastest.
Arguments:
- links: float32 [4, 18, 64, 128, 384], P(None, None, 'xy', 'zt'), may hold values from -3.4 to 3.4
- solution: float32 [6, 64, 128, 384], P(None, 'xy', 'zt'), may hold values from -6 to 6
- product: float32 [6, 64, 128, 384], P(None, 'xy', 'zt'), may hold values from -6 to 6
Outputs:
- force: float32 [4, 18, 64, 128, 384], P(None, None, 'xy', 'zt')
All inputs are finite; a program needn't handle non-finite values.
Results may differ from a plain program's by a relative error of at most 0.00002.
Values sent between devices are 32-bit elements; how exact they have to be, the bound alone decides.
No kernel may reach another device: no remote copies, remote signals or barrier semaphores. Data moves between devices by JAX's collectives and lax.ppermute only.
A program may use at most 64 MiB of HBM per device.

v0:
```python
import jax
import jax.numpy as jnp
from jax import lax
from jax.sharding import PartitionSpec as P

NT = 24


coef_one = 9.0 / 8.0
coef_naik = -1.0 / 24.0


def extended(value, sides, width):
    for axis, dim in sides:
        size, length = (lax.axis_size(axis), value.shape[dim])
        up = [(i, (i + 1) % size) for i in range(size)]
        down = [(j, i) for i, j in up]
        last = lax.slice_in_dim(value, length - width, length, axis=dim)
        initial = lax.slice_in_dim(value, 0, width, axis=dim)
        before = lax.ppermute(last, axis, up)
        after = lax.ppermute(initial, axis, down)
        value = jnp.concatenate([before, value, after], axis=dim)
    return value


def link_parts(link):
    rest = link.shape[1:]
    return (link[:9].reshape((3, 3) + rest), link[9:].reshape((3, 3) + rest))


def apply_link(link, vector):
    real_u, imag_u = link_parts(link)
    real_v, imag_v = (vector[:3], vector[3:])
    real_out = jnp.sum(real_u * real_v[None], axis=1) - jnp.sum(imag_u * imag_v[None], axis=1)
    imag_out = jnp.sum(real_u * imag_v[None], axis=1) + jnp.sum(imag_u * real_v[None], axis=1)
    return jnp.concatenate([real_out, imag_out], axis=0)


def apply_adjoint(link, vector):
    real_u, imag_u = link_parts(link)
    real_v, imag_v = (vector[:3], vector[3:])
    real_out = jnp.sum(real_u * real_v[:, None] + imag_u * imag_v[:, None], axis=0)
    imag_out = jnp.sum(real_u * imag_v[:, None] - imag_u * real_v[:, None], axis=0)
    return jnp.concatenate([real_out, imag_out], axis=0)


def outer_conj(left, right):
    real_l, imag_l = (left[:3], left[3:])
    real_r, imag_r = (right[:3], right[3:])
    rest = left.shape[1:]
    real_out = real_l[:, None] * real_r[None] + imag_l[:, None] * imag_r[None]
    imag_out = imag_l[:, None] * real_r[None] - real_l[:, None] * imag_r[None]
    return jnp.concatenate([real_out.reshape((9,) + rest), imag_out.reshape((9,) + rest)], axis=0)


def assemble(ahead_x, here_y, ahead_p2, ahead_p1, back_q1, back_q2):
    naik = (
        outer_conj(ahead_p2, here_y) + outer_conj(ahead_p1, back_q1) + outer_conj(ahead_x, back_q2)
    )
    return coef_one * outer_conj(ahead_x, here_y) + coef_naik * naik


def force_dir(link, solution, product, mover):
    ahead_x = mover(solution, 1)
    first = apply_link(link, ahead_x)
    ahead_p1 = mover(first, 1)
    second = apply_link(link, ahead_p1)
    ahead_p2 = mover(second, 1)
    back_q1 = mover(apply_adjoint(link, product), -1)
    back_q2 = mover(apply_adjoint(link, back_q1), -1)
    return assemble(ahead_x, product, ahead_p2, ahead_p1, back_q1, back_q2)


def move_time(field, step, slices):
    width = field.shape[-1]
    tpos = jnp.arange(width, dtype=jnp.int32) % slices
    if step > 0:
        return jnp.where(
            tpos < slices - step,
            jnp.roll(field, -step, axis=-1),
            jnp.roll(field, slices - step, axis=-1),
        )
    return jnp.where(
        tpos >= -step, jnp.roll(field, -step, axis=-1), jnp.roll(field, -step - slices, axis=-1)
    )


def per_device(links, solution, product):
    cells_x = solution.shape[1]
    cells_z = solution.shape[2]

    def move_y(field, step):
        return jnp.roll(field, -step * NT, axis=3)

    def move_t(field, step):
        return move_time(field, step, NT)

    force_y = force_dir(links[1], solution, product, move_y)
    force_t = force_dir(links[3], solution, product, move_t)

    def move_first(field, step):
        return jnp.roll(field, -step, axis=1)

    def move_second(field, step):
        return jnp.roll(field, -step, axis=2)

    joined_x = jnp.concatenate([links[0], solution, product], axis=0)
    wide_x = extended(joined_x, (("xy", 1),), 3)
    full_x = force_dir(wide_x[0:18], wide_x[18:24], wide_x[24:30], move_first)
    force_x = full_x[:, 3 : 3 + cells_x]
    joined_z = jnp.concatenate([links[2], solution, product], axis=0)
    wide_z = extended(joined_z, (("zt", 2),), 3)
    full_z = force_dir(wide_z[0:18], wide_z[18:24], wide_z[24:30], move_second)
    force_z = full_z[:, :, 3 : 3 + cells_z]
    return jnp.stack([force_x, force_y, force_z, force_t], axis=0)


def solution(mesh):
    placed = (P(None, None, "xy", "zt", None), P(None, "xy", "zt", None), P(None, "xy", "zt", None))
    return jax.shard_map(
        per_device,
        mesh=mesh,
        in_specs=placed,
        out_specs=P(None, None, "xy", "zt", None),
        check_vma=False,
    )
```

profile of v0, /device:TPU:1, one launch (start us, length us, event | category | flops | bytes accessed | tf_op | source)
XLA Modules:
  0.0 70.0 jit_solution(11109635073603144906)
XLA Ops:
  0.0 1.8 %slice_bitcast_fusion = (f32[18,8,4,384]{3,2,1,0:T(4,128)S(1)}, f32[1,18,8,4,384]{4,3,2,1,0:T(4,128)S(1)}) fusion(f32[4,18,8,4,384]{4,3,2,1,0:T(4,128)} %param.3), kind=kLoop, calls=%fused_computation.58 | loop fusion | bytes 3538944 | tf_op jit(solution)/shard_map/squeeze | solution.py:107
  2.1 2.1 %collective-permute-start = (f32[30,3,4,384]{3,2,1,0:T(4,128)S(1)}, f32[30,3,4,384]{3,2,1,0:T(4,128)S(1)}, u32[]{:S(2)}, u32[]{:S(2)}) collective-permute-start(f32[30,3,4,384]{3,2,1,0:T(4,128)S(1)} %get-tuple-element.81), channel_id=1, source_target_pairs={{0,32},{32,64},{64,96},{96,128},{128,160},{160,192},{192,224},{224... | collective-permute-start | bytes 1658888 | tf_op jit(solution)/shard_map/ppermute | solution.py:20
  4.2 2.5 %collective-permute-start.1 = (f32[30,3,4,384]{3,2,1,0:T(4,128)S(1)}, f32[30,3,4,384]{3,2,1,0:T(4,128)S(1)}, u32[]{:S(2)}, u32[]{:S(2)}) collective-permute-start(f32[30,3,4,384]{3,2,1,0:T(4,128)S(1)} %get-tuple-element.82), channel_id=1, source_target_pairs={{32,0},{64,32},{96,64},{128,96},{160,128},{192,160},{224,192},{0,2... | collective-permute-start | bytes 1658888 | tf_op jit(solution)/shard_map/ppermute | solution.py:21
  7.2 3.8 %collective-permute-start.2 = (f32[30,8,3,384]{3,1,2,0:T(8,128)S(1)}, f32[30,8,3,384]{3,1,2,0:T(8,128)S(1)}, u32[]{:S(2)}, u32[]{:S(2)}) collective-permute-start(f32[30,8,3,384]{3,1,2,0:T(8,128)S(1)} %get-tuple-element.83), channel_id=1, source_target_pairs={{0,1},{1,2},{2,3},{3,4},{4,5},{5,6},{6,7},{7,8},{8,9},{9,10},{10,1... | collective-permute-start | bytes 3317768 | tf_op jit(solution)/shard_map/ppermute | solution.py:20
  12.4 2.6 %multiply_add_fusion.15 = (f32[3,3,8,4,384]{4,3,2,1,0:T(4,128)S(1)}, f32[3,3,8,4,384]{4,3,2,1,0:T(4,128)S(1)}, f32[3,8,4,384]{3,2,1,0:T(4,128)S(1)}, f32[3,8,4,3...) fusion(f32[3,8,4,384]{3,2,1,0:T(4,128)S(1)} %get-tuple-element., ...), kind=kLoop, calls=%fused_computation.168 | loop fusion | flops 4423680 | bytes 6193152 | tf_op jit(solution)/shard_map/add | solution.py:51
  16.3 0.5 fusion.41
  16.8 1.0 %multiply_add_fusion.9 = (f32[3,3,8,4,384]{4,3,2,1,0:T(4,128)S(1)}, f32[3,3,8,4,384]{4,3,2,1,0:T(4,128)S(1)}, f32[3,8,4,384]{3,2,1,0:T(4,128)S(1)}, f32[3,8,4,38...) fusion(f32[3,8,4,384]{3,2,1,0:T(4,128)S(1)} %get-tuple-element., ...), kind=kLoop, calls=%fused_computation.134 | loop fusion | flops 2211840 | bytes 3244032 | tf_op jit(solution)/shard_map/add | solution.py:51
  19.9 1.0 %multiply_add_fusion.13 = (f32[3,3,8,4,384]{4,3,2,1,0:T(4,128)S(1)}, f32[3,3,8,4,384]{4,3,2,1,0:T(4,128)S(1)}, f32[3,8,4,384]{3,2,1,0:T(4,128)S(1)}, f32[3,8,4,3...) fusion(f32[3,8,4,384]{3,2,1,0:T(4,128)S(1)} %get-tuple-element., ...), kind=kLoop, calls=%fused_computation.154 | loop fusion | flops 2211840 | bytes 3244032 | tf_op jit(solution)/shard_map/add | solution.py:51
  22.0 1.8 %fusion.12 = f32[1,18,8,4,384]{4,3,2,1,0:T(4,128)} fusion(f32[1,9,8,4,384]{4,3,2,1,0:T(4,128)S(1)} %bitcast.134, f32[1,9,8,4,384]{4,3,2,1,0:T(4,128)S(1)} %bitcast.133, f32[1,9,8,4,384]{4,3,2,1,0:T(4,128)S(1)} %bitcast.146, f32[1,9,8,4,384]{4,3,2,1,0:T(4,128)S(1)} %bitcast.145, f32[1,9,8,4,384]{4,3,2,1,0:T(4,128)S(1)} %bitcast.142, ...), kind=kLoop, calls=%fused_computation.48 | loop fusion | flops 1990656 | bytes 4423680 | tf_op jit(solution)/shard_map/add | solution.py:60
  23.9 1.8 %fusion.15 = f32[1,18,8,4,384]{4,3,2,1,0:T(4,128)} fusion(f32[1,9,8,4,384]{4,3,2,1,0:T(4,128)S(1)} %bitcast.132, f32[1,9,8,4,384]{4,3,2,1,0:T(4,128)S(1)} %bitcast.131, f32[1,9,8,4,384]{4,3,2,1,0:T(4,128)S(1)} %bitcast.143, f32[1,9,8,4,384]{4,3,2,1,0:T(4,128)S(1)} %bitcast.144, f32[1,9,8,4,384]{4,3,2,1,0:T(4,128)S(1)} %bitcast.140, ...), kind=kLoop, calls=%fused_computation.53 | loop fusion | flops 1990656 | bytes 4423680 | tf_op jit(solution)/shard_map/add | solution.py:60
  25.7 3.1 %collective-permute-done = f32[30,3,4,384]{3,2,1,0:T(4,128)S(1)} collective-permute-done((f32[30,3,4,384]{3,2,1,0:T(4,128)S(1)}, f32[30,3,4,384]{3,2,1,0:T(4,128)S(1)}, u32[]{:S(2)}, u32[]{:S(2)}) %collective-permute-start) | collective-permute-done | bytes 552992 | tf_op jit(solution)/shard_map/ppermute | solution.py:20
  28.8 12.4 %collective-permute-done.1 = f32[30,3,4,384]{3,2,1,0:T(4,128)S(1)} collective-permute-done((f32[30,3,4,384]{3,2,1,0:T(4,128)S(1)}, f32[30,3,4,384]{3,2,1,0:T(4,128)S(1)}, u32[]{:S(2)}, u32[]{:S(2)}) %collective-permute-start.1) | collective-permute-done | bytes 552992 | tf_op jit(solution)/shard_map/ppermute | solution.py:21
  41.2 0.4 pad_maximum_fusion.19
  41.9 2.4 %add_reduce_fusion.3 = (f32[3,14,4,384]{3,2,1,0:T(4,128)S(1)}, f32[3,14,4,384]{3,2,1,0:T(4,128)S(1)}, f32[3,14,4,384]{3,2,1,0:T(4,128)S(1)}, f32[3,14,4,384]{3,2...) fusion(f32[3,3,14,4,384]{4,3,2,1,0:T(4,128)S(1)} %bitcast.103, ...), kind=kLoop, calls=%fused_computation.71 | loop fusion | flops 3870720 | bytes 5677056 | tf_op jit(solution)/shard_map/reduce_sum | solution.py:42
  45.0 2.2 %multiply_add_fusion.5 = (f32[3,3,14,4,384]{4,3,2,1,0:T(4,128)S(1)}, f32[3,3,14,4,384]{4,3,2,1,0:T(4,128)S(1)}, f32[3,14,4,384]{3,2,1,0:T(4,128)S(1)}, f32[3,14,...) fusion(f32[3,14,4,384]{3,2,1,0:T(4,128)S(1)} %get-tuple-element, ...), kind=kLoop, calls=%fused_computation.69 | loop fusion | flops 3870720 | bytes 5677056 | tf_op jit(solution)/shard_map/add | solution.py:51
  48.2 1.7 %fusion.8 = f32[1,18,8,4,384]{4,3,2,1,0:T(4,128)} fusion(f32[9,14,4,384]{3,2,1,0:T(4,128)S(1)} %bitcast.117, f32[9,14,4,384]{3,2,1,0:T(4,128)S(1)} %bitcast.118, f32[9,14,4,384]{3,2,1,0:T(4,128)S(1)} %bitcast.122, f32[9,14,4,384]{3,2,1,0:T(4,128)S(1)} %bitcast.121, f32[9,14,4,384]{3,2,1,0:T(4,128)S(1)} %bitcast.124, f32[9,14,4,384]{3,2,1,0:T(4,128)S(1)} %bitcast.123, ...), kind=kLoop, calls=%fused_computation.40 | loop fusion | flops 1990656 | bytes 7077888 | tf_op jit(solution)/shard_map/stack | solution.py:115
  49.9 2.3 %collective-permute-done.2 = f32[30,8,3,384]{3,1,2,0:T(8,128)S(1)} collective-permute-done((f32[30,8,3,384]{3,1,2,0:T(8,128)S(1)}, f32[30,8,3,384]{3,1,2,0:T(8,128)S(1)}, u32[]{:S(2)}, u32[]{:S(2)}) %collective-permute-start.2) | collective-permute-done | bytes 1105952 | tf_op jit(solution)/shard_map/ppermute | solution.py:20
  52.2 2.9 %collective-permute-done.3 = f32[30,8,3,384]{3,1,2,0:T(8,128)S(1)} collective-permute-done((f32[30,8,3,384]{3,1,2,0:T(8,128)S(1)}, f32[30,8,3,384]{3,1,2,0:T(8,128)S(1)}, u32[]{:S(2)}, u32[]{:S(2)}) %collective-permute-start.3) | collective-permute-done | bytes 1105952 | tf_op jit(solution)/shard_map/ppermute | solution.py:21
  55.8 0.7 add_reduce_fusion.1
  57.1 0.7 %add_reduce_fusion = (f32[3,8,10,384]{3,1,2,0:T(8,128)S(1)}, f32[3,8,10,384]{3,1,2,0:T(8,128)S(1)}, f32[3,8,10,384]{3,1,2,0:T(8,128)S(1)}, f32[3,8,10,384]{3,1,2...) fusion(f32[3,3,8,10,384]{4,2,3,1,0:T(8,128)S(1)} %bitcast.92, ...), kind=kLoop, calls=%fused_computation.16 | loop fusion | flops 3870720 | bytes 5898240 | tf_op jit(solution)/shard_map/reduce_sum | solution.py:42
  58.7 0.5 multiply_add_fusion.1
  59.2 2.9 %multiply_add_fusion.2 = (f32[3,3,8,10,384]{4,3,2,1,0:T(8,128)S(1)}, f32[3,3,8,10,384]{4,3,2,1,0:T(8,128)S(1)}, f32[3,3,8,10,384]{4,3,2,1,0:T(8,128)S(1)}, f32[3...) fusion(f32[3,8,10,384]{3,2,1,0:T(8,128)S(1)} %copy.23, ...), kind=kLoop, calls=%fused_computation.6 | loop fusion | flops 4976640 | bytes 9584640 | tf_op jit(solution)/shard_map/add | solution.py:51
  62.1 4.1 %fusion.2 = f32[1,18,8,4,384]{4,3,2,1,0:T(4,128)} fusion(f32[9,8,10,384]{3,2,1,0:T(8,128)S(1)} %bitcast.97, f32[9,8,10,384]{3,2,1,0:T(8,128)S(1)} %bitcast.98, f32[9,8,10,384]{3,2,1,0:T(8,128)} %bitcast.99, f32[9,8,10,384]{3,2,1,0:T(8,128)} %bitcast.100, f32[9,8,10,384]{3,2,1,0:T(8,128)S(1)} %bitcast.96, f32[9,8,10,384]{3,2,1,0:T(8,128)S(1)} %bitcast.95, ...), kind=kLoop, calls=%fused_computation.30 | loop fusion | flops 1990656 | bytes 9732096 | tf_op jit(solution)/shard_map/stack | solution.py:115
  66.2 3.8 %pad_maximum_fusion = f32[4,18,8,4,384]{4,3,2,1,0:T(4,128)} fusion(f32[1,18,8,4,384]{4,3,2,1,0:T(4,128)} %fusion.15, f32[1,18,8,4,384]{4,3,2,1,0:T(4,128)} %fusion.2, f32[1,18,8,4,384]{4,3,2,1,0:T(4,128)} %fusion.12, f32[1,18,8,4,384]{4,3,2,1,0:T(4,128)} %fusion.8), kind=kLoop, calls=%fused_computation | loop fusion | flops 2654208 | bytes 7077888 | tf_op jit(solution)/shard_map/stack | solution.py:115
  (113 shorter events, 10.3 us)
Async XLA Ops:
  0.0 1.8 %copy-start = (f32[6,8,4,384]{3,2,1,0:T(4,128)S(1)}, f32[6,8,4,384]{3,2,1,0:T(4,128)}, u32[]{:S(2)}) copy-start(f32[6,8,4,384]{3,2,1,0:T(4,128)} %param.4) | copy-start | bytes 884740
  0.0 1.8 %copy-start.1 = (f32[6,8,4,384]{3,2,1,0:T(4,128)S(1)}, f32[6,8,4,384]{3,2,1,0:T(4,128)}, u32[]{:S(2)}) copy-start(f32[6,8,4,384]{3,2,1,0:T(4,128)} %param.5) | copy-start | bytes 884740
  2.1 26.7 %collective-permute-start = (f32[30,3,4,384]{3,2,1,0:T(4,128)S(1)}, f32[30,3,4,384]{3,2,1,0:T(4,128)S(1)}, u32[]{:S(2)}, u32[]{:S(2)}) collective-permute-start(f32[30,3,4,384]{3,2,1,0:T(4,128)S(1)} %get-tuple-element.81), channel_id=1, source_target_pairs={{0,32},{32,64},{64,96},{96,128},{128,160},{160,192},{192,224},{224... | collective-permute-start | bytes 1658888 | tf_op jit(solution)/shard_map/ppermute | solution.py:20
  4.2 36.9 %collective-permute-start.1 = (f32[30,3,4,384]{3,2,1,0:T(4,128)S(1)}, f32[30,3,4,384]{3,2,1,0:T(4,128)S(1)}, u32[]{:S(2)}, u32[]{:S(2)}) collective-permute-start(f32[30,3,4,384]{3,2,1,0:T(4,128)S(1)} %get-tuple-element.82), channel_id=1, source_target_pairs={{32,0},{64,32},{96,64},{128,96},{160,128},{192,160},{224,192},{0,2... | collective-permute-start | bytes 1658888 | tf_op jit(solution)/shard_map/ppermute | solution.py:21
  7.0 4.6 %copy-start.2 = (f32[4,18,8,4,384]{4,3,2,1,0:T(4,128)S(1)}, f32[4,18,8,4,384]{4,3,2,1,0:T(4,128)}, u32[]{:S(2)}) copy-start(f32[4,18,8,4,384]{4,3,2,1,0:T(4,128)} %param.3) | copy-start | bytes 10616836
  7.2 45.0 %collective-permute-start.2 = (f32[30,8,3,384]{3,1,2,0:T(8,128)S(1)}, f32[30,8,3,384]{3,1,2,0:T(8,128)S(1)}, u32[]{:S(2)}, u32[]{:S(2)}) collective-permute-start(f32[30,8,3,384]{3,1,2,0:T(8,128)S(1)} %get-tuple-element.83), channel_id=1, source_target_pairs={{0,1},{1,2},{2,3},{3,4},{4,5},{5,6},{6,7},{7,8},{8,9},{9,10},{10,1... | collective-permute-start | bytes 3317768 | tf_op jit(solution)/shard_map/ppermute | solution.py:20
  10.9 44.1 %collective-permute-start.3 = (f32[30,8,3,384]{3,1,2,0:T(8,128)S(1)}, f32[30,8,3,384]{3,1,2,0:T(8,128)S(1)}, u32[]{:S(2)}, u32[]{:S(2)}) collective-permute-start(f32[30,8,3,384]{3,1,2,0:T(8,128)S(1)} %get-tuple-element.84), channel_id=1, source_target_pairs={{1,0},{2,1},{3,2},{4,3},{5,4},{6,5},{7,6},{8,7},{9,8},{10,9},{11,1... | collective-permute-start | bytes 3317768 | tf_op jit(solution)/shard_map/ppermute | solution.py:21
where the time goes:
time: 70.1 us; the launch traced here: 70 us
  other arithmetic  35.4 us (50%)
  waiting for transfers between devices  20.6 us (29%)
  starting transfers between devices  8.43 us (12%)
  local copies, waits for them, and re-layouts  4.82 us (7%)
  between operations  0.76 us (1%)
    ppermute x2, waiting for transfers between devices, extended(): after = lax.ppermute(initial, axis, down)  15.2 us
    add x11, other arithmetic, outer_conj(): real_out = real_l[:, None] * real_r[None] + imag_l[:, None] * imag_r[None]  11 us
    another operation x3, other arithmetic, per_device(): return jnp.stack([force_x, force_y, force_z, force_t], axis=0)  9.62 us
    ppermute x2, starting transfers between devices, extended(): before = lax.ppermute(last, axis, up)  5.88 us
    ppermute x2, waiting for transfers between devices, extended(): before = lax.ppermute(last, axis, up)  5.41 us
    reduce_sum x3, other arithmetic, apply_adjoint(): jnp.sum(real_u * real_v[:, None] + imag_u * imag_v[:, None], axis=0)  3.84 us
    add x2, other arithmetic, assemble(): return coef_one * outer_conj(ahead_x, here_y) + coef_naik * naik  3.52 us
    ppermute x2, starting transfers between devices, extended(): after = lax.ppermute(initial, axis, down)  2.54 us
  transfers between devices with their start and end apart: 4, of which 4 were waited for; matrix products, arithmetic and copies ran while one was open for 33% of the time, Pallas kernels for 0%

commit v1 on v0

v1 whole, which is shorter than its diff:
```python
import jax
import jax.numpy as jnp
from jax import lax
from jax.experimental import pallas as pl
from jax.experimental.pallas import tpu as pltpu
from jax.sharding import PartitionSpec as P

NT = 24
CX, CZ, YT, YB = 8, 4, 384, 3
ROWS = YB * CX * CZ

coef_one = 9.0 / 8.0
coef_naik = -1.0 / 24.0

F32 = jnp.float32


def mat_vec(u, v):
    out_r, out_i = [], []
    for a in range(3):
        re = im = None
        for b in range(3):
            ur, ui = u(3 * a + b), u(9 + 3 * a + b)
            r = ur * v[b] - ui * v[3 + b]
            i = ur * v[3 + b] + ui * v[b]
            re, im = (r, i) if re is None else (re + r, im + i)
        out_r.append(re)
        out_i.append(im)
    return out_r + out_i


def adj_vec(u, v):
    out_r, out_i = [], []
    for a in range(3):
        re = im = None
        for b in range(3):
            ur, ui = u(3 * b + a), u(9 + 3 * b + a)
            r = ur * v[b] + ui * v[3 + b]
            i = ur * v[3 + b] - ui * v[b]
            re, im = (r, i) if re is None else (re + r, im + i)
        out_r.append(re)
        out_i.append(im)
    return out_r + out_i


def store_force(put, v1, y, p1, q1, x, q2):
    for a in range(3):
        for b in range(3):
            re = im = None
            for p, q in ((v1, y), (p1, q1), (x, q2)):
                r = p[a] * q[b] + p[3 + a] * q[3 + b]
                i = p[3 + a] * q[b] - p[a] * q[3 + b]
                re, im = (r, i) if re is None else (re + r, im + i)
            put(3 * a + b, re)
            put(9 + 3 * a + b, im)


def tiles(ref):
    return ref.reshape(ref.shape[0], YB, CX, CZ, 128)


def lanes(yb):
    return pl.ds(128 * yb, 128)


def prep_kernel(links, sol, prod, zf, zb, xf, xb, ul, xs, ys, sem):
    copies = []

    def load(src, dst):
        copy = pltpu.make_async_copy(src, dst, sem.at[len(copies)])
        copy.start()
        copies.append(copy)

    ult, xst, yst = tiles(ul), tiles(xs), tiles(ys)
    for yb in range(YB):
        load(links.at[2, :, :, :, lanes(yb)], ult.at[pl.ds(18, 18), yb])
        load(sol.at[:, :, :, lanes(yb)], xst.at[:, yb])
        load(prod.at[:, :, :, lanes(yb)], yst.at[:, yb])
    for yb in range(YB):
        load(links.at[0, :, :, :, lanes(yb)], ult.at[pl.ds(0, 18), yb])
    for copy in copies[:9]:
        copy.wait()

    def layer(z):
        return pl.ds(z, YB * CX, stride=CZ)

    def uz(z):
        return lambda c: ul[18 + c, layer(z), :]

    def vec(ref, rows):
        return [ref[c, rows, :] for c in range(6)]

    p1_0 = mat_vec(uz(0), vec(xs, layer(1)))
    p2_0 = mat_vec(uz(0), mat_vec(uz(1), vec(xs, layer(2))))
    for c, value in enumerate(vec(xs, layer(0)) + p1_0 + p2_0):
        zf[c] = value
    q1 = [coef_naik * v for v in adj_vec(uz(3), vec(ys, layer(3)))]
    q2 = adj_vec(uz(3), [coef_naik * v for v in adj_vec(uz(2), vec(ys, layer(2)))])
    for c, value in enumerate(q1 + q2):
        zb[c] = value
    for copy in copies[9:]:
        copy.wait()
    for yb in range(YB):
        base = yb * CX * CZ

        def ux(row):
            return lambda c: ul[c, pl.ds(row, 8), :]

        p1 = mat_vec(ux(base), vec(xs, pl.ds(base + CZ, 8)))
        p2 = mat_vec(ux(base), [pltpu.roll(v, 4, 0) for v in p1])
        for c, value in enumerate(vec(xs, pl.ds(base, 8)) + p1 + p2):
            xf[c, yb] = value[:CZ]
        last = base + (CX - 2) * CZ
        w1 = [coef_naik * v for v in adj_vec(ux(last), vec(ys, pl.ds(last, 8)))]
        w2 = adj_vec(ux(last), [pltpu.roll(v, 4, 0) for v in w1])
        for c, value in enumerate(w1 + w2):
            xb[c, yb] = value[CZ:]


def move_y(v, step):
    lane = lax.broadcasted_iota(jnp.int32, (8, 128), 1)
    if step > 0:
        r = [pltpu.roll(a, 128 - NT, 1) for a in v]
        return [jnp.where(lane < 128 - NT, r[k], r[(k + 1) % YB]) for k in range(YB)]
    r = [pltpu.roll(a, NT, 1) for a in v]
    return [jnp.where(lane >= NT, r[k], r[(k - 1) % YB]) for k in range(YB)]


def move_t(v, step):
    lane = lax.broadcasted_iota(jnp.int32, (8, 128), 1)
    out = []
    if step > 0:
        near = [pltpu.roll(a, 127, 1) for a in v]
        wrap = [pltpu.roll(a, NT - 1, 1) for a in v]
        for k in range(YB):
            edge = (lane + 128 * k) % NT == NT - 1
            far = wrap[k] if k == 0 else jnp.where(lane < NT - 1, wrap[k - 1], wrap[k])
            beside = near[k] if k == YB - 1 else jnp.where(lane == 127, near[k + 1], near[k])
            out.append(jnp.where(edge, far, beside))
        return out
    near = [pltpu.roll(a, 1, 1) for a in v]
    wrap = [pltpu.roll(a, 128 - (NT - 1), 1) for a in v]
    for k in range(YB):
        edge = (lane + 128 * k) % NT == 0
        far = wrap[k] if k == YB - 1 else jnp.where(lane >= 128 - (NT - 1), wrap[k + 1], wrap[k])
        beside = near[k] if k == 0 else jnp.where(lane == 0, near[k - 1], near[k])
        out.append(jnp.where(edge, far, beside))
    return out


def local_kernel(links, xs, ys, force, ul, fs, sem_in, sem_out):
    ult, fst = tiles(ul), tiles(fs)
    loads = []
    for d, mu in enumerate((1, 3)):
        for yb in range(YB):
            copy = pltpu.make_async_copy(
                links.at[mu, :, :, :, lanes(yb)],
                ult.at[pl.ds(18 * d, 18), yb],
                sem_in.at[d * YB + yb],
            )
            copy.start()
            loads.append(copy)

    def out_copy(d, mu, yb, xp):
        return pltpu.make_async_copy(
            fst.at[pl.ds(18 * d, 18), yb, pl.ds(2 * xp, 2)],
            force.at[mu, :, pl.ds(2 * xp, 2), :, lanes(yb)],
            sem_out.at[(d * YB + yb) * 4 + xp],
        )

    for d, (mu, move) in enumerate(((1, move_y), (3, move_t))):
        for copy in loads[d * YB : (d + 1) * YB]:
            copy.wait()

        def body(xp, carry):
            rows = [pl.ds(pl.multiple_of(yb * CX * CZ + xp * 8, 8), 8) for yb in range(YB)]

            def shift(vecs, step):
                moved = [move([vecs[k][c] for k in range(YB)], step) for c in range(6)]
                return [[moved[c][k] for c in range(6)] for k in range(YB)]

            def u(k):
                return lambda c: ul[18 * d + c, rows[k], :]

            def vec(ref):
                return [[ref[c, rows[k], :] for c in range(6)] for k in range(YB)]

            x = shift(vec(xs), 1)
            p1 = shift([mat_vec(u(k), x[k]) for k in range(YB)], 1)
            p2 = shift([mat_vec(u(k), p1[k]) for k in range(YB)], 1)
            v1 = [[coef_one * a + coef_naik * b for a, b in zip(x[k], p2[k])] for k in range(YB)]
            y = vec(ys)
            q1 = [adj_vec(u(k), y[k]) for k in range(YB)]
            q1 = shift([[coef_naik * a for a in v] for v in q1], -1)
            q2 = shift([adj_vec(u(k), q1[k]) for k in range(YB)], -1)
            for k in range(YB):

                def put(c, value, k=k):
                    fs[18 * d + c, rows[k], :] = value

                store_force(put, v1[k], y[k], p1[k], q1[k], x[k], q2[k])
            for yb in range(YB):
                out_copy(d, mu, yb, xp).start()
            return carry

        lax.fori_loop(0, 4, body, 0)
    for d, mu in enumerate((1, 3)):
        for yb in range(YB):
            for xp in range(4):
                out_copy(d, mu, yb, xp).wait()


def edge_kernel(zf, zb, xf, xb, ul, xs, ys, _, force, fs, hz, hx, sem_out):
    fst = tiles(fs)
    row = lax.broadcasted_iota(jnp.int32, (8, 128), 0)

    for c in range(18):
        hz[c, pl.ds(CZ - 1, YB * CX, stride=CZ), :] = zf[c]
    for c in range(12):
        hz[c, pl.ds(0, YB * CX, stride=CZ), :] = zb[c]

    def out_z(yb):
        return pltpu.make_async_copy(
            fst.at[pl.ds(18, 18), yb], force.at[2, :, :, :, lanes(yb)], sem_out.at[yb]
        )

    def out_x(yb):
        return pltpu.make_async_copy(
            fst.at[pl.ds(0, 18), yb], force.at[0, :, :, :, lanes(yb)], sem_out.at[YB + yb]
        )

    def body_z(xp, yb):
        rows = pl.ds(pl.multiple_of(yb * CX * CZ + xp * 8, 8), 8)
        top, bottom = row % CZ == CZ - 1, row % CZ == 0

        def vec(ref, first=0):
            return [ref[first + c, rows, :] for c in range(6)]

        def ahead(v, first):
            return [jnp.where(top, h, pltpu.roll(a, 7, 0)) for a, h in zip(v, vec(hz, first))]

        def back(v, first):
            return [jnp.where(bottom, h, pltpu.roll(a, 1, 0)) for a, h in zip(v, vec(hz, first))]

        def u(c):
            return ul[18 + c, rows, :]

        x = ahead(vec(xs), 0)
        p1 = ahead(mat_vec(u, x), 6)
        p2 = ahead(mat_vec(u, p1), 12)
        v1 = [coef_one * a + coef_naik * b for a, b in zip(x, p2)]
        y = vec(ys)
        q1 = back([coef_naik * a for a in adj_vec(u, y)], 0)
        q2 = back(adj_vec(u, q1), 6)

        def put(c, value):
            fs[18 + c, rows, :] = value

        store_force(put, v1, y, p1, q1, x, q2)
        return yb

    for yb in range(YB):
        lax.fori_loop(0, 4, body_z, yb)
        out_z(yb).start()

    for yb in range(YB):
        for c in range(18):
            hx[c, pl.ds(yb * 8 + CZ, CZ), :] = xf[c, yb]
        for c in range(12):
            hx[c, pl.ds(yb * 8, CZ), :] = xb[c, yb]

    def body_x(yb, carry):
        rows = [pl.ds(pl.multiple_of(yb * CX * CZ + k * 8, 8), 8) for k in range(4)]
        edge = pl.ds(pl.multiple_of(yb * 8, 8), 8)
        low = row < CZ

        def vec(ref):
            return [[ref[c, rows[k], :] for c in range(6)] for k in range(4)]

        def half(vecs):
            return [[pltpu.roll(a, CZ, 0) for a in v] for v in vecs]

        def ahead(vecs, first):
            r = half(vecs) + [[hx[first + c, edge, :] for c in range(6)]]
            return [[jnp.where(low, a, b) for a, b in zip(r[k], r[k + 1])] for k in range(4)]

        def back(vecs, first):
            r = [[hx[first + c, edge, :] for c in range(6)]] + half(vecs)
            return [[jnp.where(low, a, b) for a, b in zip(r[k], r[k + 1])] for k in range(4)]

        def u(k):
            return lambda c: ul[c, rows[k], :]

        x = ahead(vec(xs), 0)
        p1 = ahead([mat_vec(u(k), x[k]) for k in range(4)], 6)
        p2 = ahead([mat_vec(u(k), p1[k]) for k in range(4)], 12)
        v1 = [[coef_one * a + coef_naik * b for a, b in zip(x[k], p2[k])] for k in range(4)]
        y = vec(ys)
        q1 = back([[coef_naik * a for a in adj_vec(u(k), y[k])] for k in range(4)], 0)
        q2 = back([adj_vec(u(k), q1[k]) for k in range(4)], 6)
        for k in range(4):

            def put(c, value, k=k):
                fs[c, rows[k], :] = value

            store_force(put, v1[k], y[k], p1[k], q1[k], x[k], q2[k])
        out_x(yb).start()
        return carry

    lax.fori_loop(0, YB, body_x, 0)
    for yb in range(YB):
        out_z(yb).wait()
        out_x(yb).wait()


HBM = pl.BlockSpec(memory_space=pltpu.HBM)
VM = pl.BlockSpec(memory_space=pltpu.VMEM)
MIB = 1 << 20


def per_device(links, solution, product):
    links, solution, product = (
        pltpu.with_memory_space_constraint(a, pltpu.HBM) for a in (links, solution, product)
    )
    zf, zb, xf, xb, ul, xs, ys = pl.pallas_call(
        prep_kernel,
        out_shape=(
            pltpu.VMEM((18, YB * CX, 128), F32),
            pltpu.VMEM((12, YB * CX, 128), F32),
            pltpu.VMEM((18, YB, CZ, 128), F32),
            pltpu.VMEM((12, YB, CZ, 128), F32),
            pltpu.VMEM((36, ROWS, 128), F32),
            pltpu.VMEM((6, ROWS, 128), F32),
            pltpu.VMEM((6, ROWS, 128), F32),
        ),
        in_specs=[HBM] * 3,
        out_specs=[VM] * 7,
        scratch_shapes=[pltpu.SemaphoreType.DMA((12,))],
        cost_estimate=pl.CostEstimate(flops=4000000, bytes_accessed=5000000, transcendentals=0),
        compiler_params=pltpu.CompilerParams(vmem_limit_bytes=16 * MIB),
        name="prep",
    )(links, solution, product)

    def ring(axis):
        size = lax.axis_size(axis)
        up = [(i, (i + 1) % size) for i in range(size)]
        return up, [(j, i) for i, j in up]

    up_z, down_z = ring("zt")
    up_x, down_x = ring("xy")
    zf = lax.ppermute(zf, "zt", down_z)
    zb = lax.ppermute(zb, "zt", up_z)
    xf = lax.ppermute(xf, "xy", down_x)
    xb = lax.ppermute(xb, "xy", up_x)

    force_shape = jax.ShapeDtypeStruct((4, 18, CX, CZ, YT), F32)
    force = pl.pallas_call(
        local_kernel,
        out_shape=force_shape,
        in_specs=[HBM, VM, VM],
        out_specs=HBM,
        scratch_shapes=[
            pltpu.VMEM((36, ROWS, 128), F32),
            pltpu.VMEM((36, ROWS, 128), F32),
            pltpu.SemaphoreType.DMA((6,)),
            pltpu.SemaphoreType.DMA((24,)),
        ],
        cost_estimate=pl.CostEstimate(flops=12000000, bytes_accessed=12000000, transcendentals=0),
        compiler_params=pltpu.CompilerParams(vmem_limit_bytes=16 * MIB),
        name="local",
    )(links, xs, ys)
    return pl.pallas_call(
        edge_kernel,
        out_shape=force_shape,
        in_specs=[VM] * 7 + [HBM],
        out_specs=HBM,
        input_output_aliases={7: 0},
        scratch_shapes=[
            pltpu.VMEM((36, ROWS, 128), F32),
            pltpu.VMEM((18, ROWS, 128), F32),
            pltpu.VMEM((18, YB * 8, 128), F32),
            pltpu.SemaphoreType.DMA((6,)),
        ],
        cost_estimate=pl.CostEstimate(flops=12000000, bytes_accessed=12000000, transcendentals=0),
        compiler_params=pltpu.CompilerParams(vmem_limit_bytes=16 * MIB),
        name="edge",
    )(zf, zb, xf, xb, ul, xs, ys, force)


def solution(mesh):
    placed = (P(None, None, "xy", "zt", None), P(None, "xy", "zt", None), P(None, "xy", "zt", None))
    return jax.shard_map(
        per_device,
        mesh=mesh,
        in_specs=placed,
        out_specs=P(None, None, "xy", "zt", None),
        check_vma=False,
    )
```

time: 70.1 us -> 21.1 us (0.30)
  the two profiles are of different devices: /device:TPU:1 before, /device:TPU:26 now
where the time goes in v1:
time: 21.1 us; the launch traced here: 21 us
  starting transfers between devices  11.1 us (53%)
  Pallas kernels  9.86 us (47%)
    ppermute x1, starting transfers between devices, per_device(): zf = lax.ppermute(zf, 'zt', down_z)  6.93 us
    pallas_call x1, Pallas kernels, per_device(): pl.pallas_call(local_kernel, out_shape=force_shape, in_specs=[HBM, VM, VM...  5.22 us
    pallas_call x1, Pallas kernels, per_device(): pl.pallas_call(edge_kernel, out_shape=force_shape, in_specs=[VM] * 7 + [H...  2.8 us
    ppermute x1, starting transfers between devices, per_device(): xb = lax.ppermute(xb, 'xy', up_x)  2.7 us
    pallas_call x1, Pallas kernels, per_device(): pl.pallas_call(prep_kernel, out_shape=(pltpu.VMEM((18, YB * CX, 128), F32...  1.85 us
    ppermute x1, starting transfers between devices, per_device(): xf = lax.ppermute(xf, 'xy', down_x)  1.43 us
  transfers between devices with their start and end apart: 4, of which 0 were waited for; matrix products, arithmetic and copies ran while one was open for 0% of the time, Pallas kernels for 25%

profile of v1, /device:TPU:26, one launch (start us, length us, event | category | flops | bytes accessed | tf_op | source)
XLA Modules:
  0.0 21.0 jit_solution(16546322339955309362)
XLA Ops:
  0.0 1.8 %prep.1 = (f32[18,24,128]{2,1,0:T(8,128)S(1)}, f32[12,24,128]{2,1,0:T(8,128)S(1)}, f32[18,3,4,128]{3,2,1,0:T(4,128)S(1)}, f32[12,3,4,128]{3,2,1,0:T(4,128)S(1)},...) custom-call(f32[4,18,8,4,384]{4,3,2,1,0:T(4,128)} %links.3, ...), custom_call_target="tpu_custom_call" | custom-call | flops 4000000 | bytes 5000000 | tf_op jit(solution)/shard_map/prep/pallas_call | solution.py:325
  1.9 6.9 %collective-permute-start = (f32[18,24,128]{2,1,0:T(8,128)S(1)}, f32[18,24,128]{2,1,0:T(8,128)S(1)}, u32[]{:S(2)}, u32[]{:S(2)}) collective-permute-start(f32[18,24,128]{2,1,0:T(8,128)S(1)} %get-tuple-element.12), channel_id=1, source_target_pairs={{1,0},{2,1},{3,2},{4,3},{5,4},{6,5},{7,6},{8,7},{9,8},{10,9},{11,1... | collective-permute-start | bytes 663560 | tf_op jit(solution)/shard_map/ppermute | solution.py:351
  8.8 0.0 collective-permute-start.1
  8.8 1.4 %collective-permute-start.2 = (f32[18,3,4,128]{3,2,1,0:T(4,128)S(1)}, f32[18,3,4,128]{3,2,1,0:T(4,128)S(1)}, u32[]{:S(2)}, u32[]{:S(2)}) collective-permute-start(f32[18,3,4,128]{3,2,1,0:T(4,128)S(1)} %get-tuple-element.14), channel_id=1, source_target_pairs={{32,0},{64,32},{96,64},{128,96},{160,128},{192,160},{224,192},{0,2... | collective-permute-start | bytes 331784 | tf_op jit(solution)/shard_map/ppermute | solution.py:353
  10.2 2.7 %collective-permute-start.3 = (f32[12,3,4,128]{3,2,1,0:T(4,128)S(1)}, f32[12,3,4,128]{3,2,1,0:T(4,128)S(1)}, u32[]{:S(2)}, u32[]{:S(2)}) collective-permute-start(f32[12,3,4,128]{3,2,1,0:T(4,128)S(1)} %get-tuple-element.15), channel_id=1, source_target_pairs={{0,32},{32,64},{64,96},{96,128},{128,160},{160,192},{192,224},{224... | collective-permute-start | bytes 221192 | tf_op jit(solution)/shard_map/ppermute | solution.py:354
  12.9 5.2 %local.1._ = f32[4,18,8,4,384]{4,3,2,1,0:T(4,128)} custom-call(f32[4,18,8,4,384]{4,3,2,1,0:T(4,128)} %links.3, f32[6,96,128]{2,1,0:T(8,128)S(1)} %get-tuple-element.17.xs, f32[6,96,128]{2,1,0:T(8,128)S(1)} %get-tuple-element.18.ys), custom_call_target="tpu_custom_call" | custom-call | flops 12000000 | bytes 12000000 | tf_op jit(solution)/shard_map/local/pallas_call | solution.py:357
  18.2 0.0 collective-permute-done.3.xb
  18.2 0.0 collective-permute-done.2.xf
  18.2 0.0 collective-permute-done.1.zb
  18.2 0.0 collective-permute-done.zf
  18.2 2.8 %edge.1 = f32[4,18,8,4,384]{4,3,2,1,0:T(4,128)} custom-call(f32[18,24,128]{2,1,0:T(8,128)S(1)} %collective-permute-done.zf, f32[12,24,128]{2,1,0:T(8,128)S(1)} %collective-permute-done.1.zb, f32[18,3,4,128]{3,2,1,0:T(4,128)S(1)} %collective-permute-done.2.xf, f32[12,3,4,128]{3,2,1,0:T(4,128)S(1)} %collective-permute-done.3.xb, ...), custom_call_target="tpu_custom_call", output_to_operand_aliasing={{}: (7, {})} | custom-call | flops 12000000 | bytes 12000000 | tf_op jit(solution)/shard_map/edge/pallas_call | solution.py:372
Async XLA Ops:
  1.9 16.3 %collective-permute-start = (f32[18,24,128]{2,1,0:T(8,128)S(1)}, f32[18,24,128]{2,1,0:T(8,128)S(1)}, u32[]{:S(2)}, u32[]{:S(2)}) collective-permute-start(f32[18,24,128]{2,1,0:T(8,128)S(1)} %get-tuple-element.12), channel_id=1, source_target_pairs={{1,0},{2,1},{3,2},{4,3},{5,4},{6,5},{7,6},{8,7},{9,8},{10,9},{11,1... | collective-permute-start | bytes 663560 | tf_op jit(solution)/shard_map/ppermute | solution.py:351
  8.8 9.4 %collective-permute-start.1 = (f32[12,24,128]{2,1,0:T(8,128)S(1)}, f32[12,24,128]{2,1,0:T(8,128)S(1)}, u32[]{:S(2)}, u32[]{:S(2)}) collective-permute-start(f32[12,24,128]{2,1,0:T(8,128)S(1)} %get-tuple-element.13), channel_id=1, source_target_pairs={{0,1},{1,2},{2,3},{3,4},{4,5},{5,6},{6,7},{7,8},{8,9},{9,10},{10,1... | collective-permute-start | bytes 442376 | tf_op jit(solution)/shard_map/ppermute | solution.py:352
  8.8 9.4 %collective-permute-start.2 = (f32[18,3,4,128]{3,2,1,0:T(4,128)S(1)}, f32[18,3,4,128]{3,2,1,0:T(4,128)S(1)}, u32[]{:S(2)}, u32[]{:S(2)}) collective-permute-start(f32[18,3,4,128]{3,2,1,0:T(4,128)S(1)} %get-tuple-element.14), channel_id=1, source_target_pairs={{32,0},{64,32},{96,64},{128,96},{160,128},{192,160},{224,192},{0,2... | collective-permute-start | bytes 331784 | tf_op jit(solution)/shard_map/ppermute | solution.py:353
  10.2 7.9 %collective-permute-start.3 = (f32[12,3,4,128]{3,2,1,0:T(4,128)S(1)}, f32[12,3,4,128]{3,2,1,0:T(4,128)S(1)}, u32[]{:S(2)}, u32[]{:S(2)}) collective-permute-start(f32[12,3,4,128]{3,2,1,0:T(4,128)S(1)} %get-tuple-element.15), channel_id=1, source_target_pairs={{0,32},{32,64},{64,96},{96,128},{128,160},{160,192},{192,224},{224... | collective-permute-start | bytes 221192 | tf_op jit(solution)/shard_map/ppermute | solution.py:354

commit v2 on v1

v2 whole, which is shorter than its diff:
```python
import jax
import jax.numpy as jnp
from jax import lax
from jax.experimental import pallas as pl
from jax.experimental.pallas import tpu as pltpu
from jax.sharding import PartitionSpec as P

NT = 24
CX, CZ, YT, YB = 8, 4, 384, 3
ROWS = YB * CX * CZ

coef_one = 9.0 / 8.0
coef_naik = -1.0 / 24.0

F32 = jnp.float32


def mat_vec(u, v):
    out_r, out_i = [], []
    for a in range(3):
        re = im = None
        for b in range(3):
            ur, ui = u(3 * a + b), u(9 + 3 * a + b)
            r = ur * v[b] - ui * v[3 + b]
            i = ur * v[3 + b] + ui * v[b]
            re, im = (r, i) if re is None else (re + r, im + i)
        out_r.append(re)
        out_i.append(im)
    return out_r + out_i


def adj_vec(u, v):
    out_r, out_i = [], []
    for a in range(3):
        re = im = None
        for b in range(3):
            ur, ui = u(3 * b + a), u(9 + 3 * b + a)
            r = ur * v[b] + ui * v[3 + b]
            i = ur * v[3 + b] - ui * v[b]
            re, im = (r, i) if re is None else (re + r, im + i)
        out_r.append(re)
        out_i.append(im)
    return out_r + out_i


def store_force(put, v1, y, p1, q1, x, q2):
    for a in range(3):
        for b in range(3):
            re = im = None
            for p, q in ((v1, y), (p1, q1), (x, q2)):
                r = p[a] * q[b] + p[3 + a] * q[3 + b]
                i = p[3 + a] * q[b] - p[a] * q[3 + b]
                re, im = (r, i) if re is None else (re + r, im + i)
            put(3 * a + b, re)
            put(9 + 3 * a + b, im)


def tiles(ref):
    return ref.reshape(ref.shape[0], YB, CX, CZ, 128)


def lanes(yb):
    return pl.ds(128 * yb, 128)


class Loads:
    def __init__(self, sem):
        self.sem, self.copies, self.count = sem, {}, 0

    def start(self, name, src, dst):
        copy = pltpu.make_async_copy(src, dst, self.sem.at[self.count])
        copy.start()
        self.copies.setdefault(name, []).append(copy)
        self.count += 1

    def wait(self, name):
        for copy in self.copies.pop(name):
            copy.wait()


def vector(ref, rows, first=0):
    return [ref[first + c, rows, :] for c in range(6)]


def prep_kernel(links, sol, prod, xf, xb, ux, xs, ys, sem):
    loads = Loads(sem)
    uxt, xst, yst = tiles(ux), tiles(xs), tiles(ys)

    def load_x(name, first, count):
        for yb in range(YB):
            loads.start(
                name,
                links.at[0, :, pl.ds(first, count), :, lanes(yb)],
                uxt.at[:, yb, pl.ds(first, count)],
            )

    for yb in range(YB):
        loads.start("y", prod.at[:, :, :, lanes(yb)], yst.at[:, yb])
    load_x("last", CX - 2, 2)
    for yb in range(YB):
        loads.start("x", sol.at[:, :, :, lanes(yb)], xst.at[:, yb])
    load_x("first", 0, 2)
    load_x("inner", 2, CX - 4)

    def u(row):
        return lambda c: ux[c, pl.ds(row, 8), :]

    loads.wait("y")
    loads.wait("last")
    for yb in range(YB):
        last = yb * CX * CZ + (CX - 2) * CZ
        w1 = [coef_naik * v for v in adj_vec(u(last), vector(ys, pl.ds(last, 8)))]
        w2 = adj_vec(u(last), [pltpu.roll(v, 4, 0) for v in w1])
        for c, value in enumerate(w1 + w2):
            xb[c, yb] = value[CZ:]
    loads.wait("x")
    loads.wait("first")
    for yb in range(YB):
        base = yb * CX * CZ
        p1 = mat_vec(u(base), vector(xs, pl.ds(base + CZ, 8)))
        p2 = mat_vec(u(base), [pltpu.roll(v, 4, 0) for v in p1])
        for c, value in enumerate(vector(xs, pl.ds(base, 8)) + p1 + p2):
            xf[c, yb] = value[:CZ]
    loads.wait("inner")


def move_y(v, step):
    lane = lax.broadcasted_iota(jnp.int32, (8, 128), 1)
    if step > 0:
        r = [pltpu.roll(a, 128 - NT, 1) for a in v]
        return [jnp.where(lane < 128 - NT, r[k], r[(k + 1) % YB]) for k in range(YB)]
    r = [pltpu.roll(a, NT, 1) for a in v]
    return [jnp.where(lane >= NT, r[k], r[(k - 1) % YB]) for k in range(YB)]


def move_t(v, step):
    lane = lax.broadcasted_iota(jnp.int32, (8, 128), 1)
    out = []
    if step > 0:
        near = [pltpu.roll(a, 127, 1) for a in v]
        wrap = [pltpu.roll(a, NT - 1, 1) for a in v]
        for k in range(YB):
            edge = (lane + 128 * k) % NT == NT - 1
            far = wrap[k] if k == 0 else jnp.where(lane < NT - 1, wrap[k - 1], wrap[k])
            beside = near[k] if k == YB - 1 else jnp.where(lane == 127, near[k + 1], near[k])
            out.append(jnp.where(edge, far, beside))
        return out
    near = [pltpu.roll(a, 1, 1) for a in v]
    wrap = [pltpu.roll(a, 128 - (NT - 1), 1) for a in v]
    for k in range(YB):
        edge = (lane + 128 * k) % NT == 0
        far = wrap[k] if k == YB - 1 else jnp.where(lane >= 128 - (NT - 1), wrap[k + 1], wrap[k])
        beside = near[k] if k == 0 else jnp.where(lane == 0, near[k - 1], near[k])
        out.append(jnp.where(edge, far, beside))
    return out


def share():
    at = lax.axis_index("zt")
    return jnp.where(at == 0, 8, jnp.where(at == lax.axis_size("zt") - 1, 0, 4))


def local_piece(d, piece, move, ul, xs, ys, fs):
    rows = [pl.ds(pl.multiple_of(yb * CX * CZ + piece * 8, 8), 8) for yb in range(YB)]

    def shift(vecs, step):
        moved = [move([vecs[k][c] for k in range(YB)], step) for c in range(6)]
        return [[moved[c][k] for c in range(6)] for k in range(YB)]

    def u(k):
        return lambda c: ul[18 * (d + 1) + c, rows[k], :]

    x = shift([vector(xs, r) for r in rows], 1)
    p1 = shift([mat_vec(u(k), x[k]) for k in range(YB)], 1)
    p2 = shift([mat_vec(u(k), p1[k]) for k in range(YB)], 1)
    v1 = [[coef_one * a + coef_naik * b for a, b in zip(x[k], p2[k])] for k in range(YB)]
    y = [vector(ys, r) for r in rows]
    q1 = [adj_vec(u(k), y[k]) for k in range(YB)]
    q1 = shift([[coef_naik * a for a in v] for v in q1], -1)
    q2 = shift([adj_vec(u(k), q1[k]) for k in range(YB)], -1)
    for k in range(YB):

        def put(c, value, k=k):
            fs[18 * d + c, rows[k], :] = value

        store_force(put, v1[k], y[k], p1[k], q1[k], x[k], q2[k])


def early_kernel(links, xs, ys, zf, zb, ul, fs, sem):
    loads = Loads(sem)
    ult = tiles(ul)
    for d, mu in enumerate((2, 1, 3)):
        for yb in range(YB):
            loads.start(mu, links.at[mu, :, :, :, lanes(yb)], ult.at[pl.ds(18 * d, 18), yb])

    def layer(z):
        return pl.ds(z, YB * CX, stride=CZ)

    def u(z):
        return lambda c: ul[c, layer(z), :]

    loads.wait(2)
    q1 = [coef_naik * v for v in adj_vec(u(3), vector(ys, layer(3)))]
    q2 = adj_vec(u(3), [coef_naik * v for v in adj_vec(u(2), vector(ys, layer(2)))])
    for c, value in enumerate(q1 + q2):
        zb[c] = value
    p1 = mat_vec(u(0), vector(xs, layer(1)))
    p2 = mat_vec(u(0), mat_vec(u(1), vector(xs, layer(2))))
    for c, value in enumerate(vector(xs, layer(0)) + p1 + p2):
        zf[c] = value

    count = share()
    for d, (mu, move) in enumerate(((1, move_y), (3, move_t))):
        loads.wait(mu)

        def body(piece, carry):
            local_piece(d, piece, move, ul, xs, ys, fs)
            return carry

        lax.fori_loop(0, jnp.clip(count - 4 * d, 0, 4), body, 0)


def late_kernel(ul, xs, ys, done, force, fs, sem):
    count = share()

    def out_copy(src, d, piece, yb):
        return pltpu.make_async_copy(
            tiles(src).at[pl.ds(18 * d, 18), yb, pl.ds(2 * piece, 2)],
            force.at[2 * d + 1, :, pl.ds(2 * piece, 2), :, lanes(yb)],
            sem.at[(d * YB + yb) * 4 + piece],
        )

    for d, move in enumerate((move_y, move_t)):
        split = jnp.clip(count - 4 * d, 0, 4)

        def send(piece, carry):
            for yb in range(YB):
                out_copy(done, d, piece, yb).start()
            return carry

        def body(piece, carry):
            local_piece(d, piece, move, ul, xs, ys, fs)
            for yb in range(YB):
                out_copy(fs, d, piece, yb).start()
            return carry

        lax.fori_loop(0, split, send, 0)
        lax.fori_loop(split, 4, body, 0)
    for d in range(2):
        for yb in range(YB):
            for piece in range(4):
                out_copy(fs, d, piece, yb).wait()


def edge_x_kernel(xf, xb, ux, xs, ys, fx, hx):
    low = lax.broadcasted_iota(jnp.int32, (8, 128), 0) < CZ
    for yb in range(YB):
        for c in range(18):
            hx[c, pl.ds(yb * 8 + CZ, CZ), :] = xf[c, yb]
        for c in range(12):
            hx[c, pl.ds(yb * 8, CZ), :] = xb[c, yb]

    def body(yb, carry):
        rows = [pl.ds(pl.multiple_of(yb * CX * CZ + k * 8, 8), 8) for k in range(4)]
        edge = pl.ds(pl.multiple_of(yb * 8, 8), 8)

        def half(vecs):
            return [[pltpu.roll(a, CZ, 0) for a in v] for v in vecs]

        def joined(r):
            return [[jnp.where(low, a, b) for a, b in zip(r[k], r[k + 1])] for k in range(4)]

        def ahead(vecs, first):
            return joined(half(vecs) + [vector(hx, edge, first)])

        def back(vecs, first):
            return joined([vector(hx, edge, first)] + half(vecs))

        def u(k):
            return lambda c: ux[c, rows[k], :]

        x = ahead([vector(xs, r) for r in rows], 0)
        p1 = ahead([mat_vec(u(k), x[k]) for k in range(4)], 6)
        p2 = ahead([mat_vec(u(k), p1[k]) for k in range(4)], 12)
        v1 = [[coef_one * a + coef_naik * b for a, b in zip(x[k], p2[k])] for k in range(4)]
        y = [vector(ys, r) for r in rows]
        q1 = back([[coef_naik * a for a in adj_vec(u(k), y[k])] for k in range(4)], 0)
        q2 = back([adj_vec(u(k), q1[k]) for k in range(4)], 6)
        for k in range(4):

            def put(c, value, k=k):
                fx[c, rows[k], :] = value

            store_force(put, v1[k], y[k], p1[k], q1[k], x[k], q2[k])
        return carry

    lax.fori_loop(0, YB, body, 0)


def edge_z_kernel(zf, zb, ul, xs, ys, fx, _, force, fz, hz, sem):
    def out_copy(src, mu, yb):
        return pltpu.make_async_copy(
            tiles(src).at[:, yb], force.at[mu, :, :, :, lanes(yb)], sem.at[mu + yb * 4]
        )

    for yb in range(YB):
        out_copy(fx, 0, yb).start()
    for c in range(18):
        hz[c, pl.ds(CZ - 1, YB * CX, stride=CZ), :] = zf[c]
    for c in range(12):
        hz[c, pl.ds(0, YB * CX, stride=CZ), :] = zb[c]
    row = lax.broadcasted_iota(jnp.int32, (8, 128), 0)
    top, bottom = row % CZ == CZ - 1, row % CZ == 0

    def body(piece, yb):
        rows = pl.ds(pl.multiple_of(yb * CX * CZ + piece * 8, 8), 8)

        def ahead(v, first):
            halo = vector(hz, rows, first)
            return [jnp.where(top, h, pltpu.roll(a, 7, 0)) for a, h in zip(v, halo)]

        def back(v, first):
            halo = vector(hz, rows, first)
            return [jnp.where(bottom, h, pltpu.roll(a, 1, 0)) for a, h in zip(v, halo)]

        def u(c):
            return ul[c, rows, :]

        x = ahead(vector(xs, rows), 0)
        p1 = ahead(mat_vec(u, x), 6)
        p2 = ahead(mat_vec(u, p1), 12)
        v1 = [coef_one * a + coef_naik * b for a, b in zip(x, p2)]
        y = vector(ys, rows)
        q1 = back([coef_naik * a for a in adj_vec(u, y)], 0)
        q2 = back(adj_vec(u, q1), 6)

        def put(c, value):
            fz[c, rows, :] = value

        store_force(put, v1, y, p1, q1, x, q2)
        return yb

    for yb in range(YB):
        lax.fori_loop(0, 4, body, yb)
        out_copy(fz, 2, yb).start()
    for yb in range(YB):
        out_copy(fx, 0, yb).wait()
        out_copy(fz, 2, yb).wait()


HBM = pl.BlockSpec(memory_space=pltpu.HBM)
VM = pl.BlockSpec(memory_space=pltpu.VMEM)
FORCE = jax.ShapeDtypeStruct((4, 18, CX, CZ, YT), F32)


def held(*shape):
    return pltpu.VMEM(shape, F32)


def kernel_call(body, name, flops, **args):
    return pl.pallas_call(
        body,
        name=name,
        cost_estimate=pl.CostEstimate(flops=flops, bytes_accessed=flops, transcendentals=0),
        compiler_params=pltpu.CompilerParams(vmem_limit_bytes=16 << 20),
        **args,
    )


def shifted(value, axis, step):
    size = lax.axis_size(axis)
    return lax.ppermute(value, axis, [(i, (i + step) % size) for i in range(size)])


def per_device(links, solution, product):
    links, solution, product = (
        pltpu.with_memory_space_constraint(a, pltpu.HBM) for a in (links, solution, product)
    )
    dma = pltpu.SemaphoreType.DMA
    xf, xb, ux, xs, ys = kernel_call(
        prep_kernel,
        "prep",
        3000000,
        out_shape=(
            held(18, YB, CZ, 128),
            held(12, YB, CZ, 128),
            held(18, ROWS, 128),
            held(6, ROWS, 128),
            held(6, ROWS, 128),
        ),
        in_specs=[HBM] * 3,
        out_specs=[VM] * 5,
        scratch_shapes=[dma((15,))],
    )(links, solution, product)
    xb = shifted(xb, "xy", 1)
    xf = shifted(xf, "xy", -1)
    zf, zb, ul, done = kernel_call(
        early_kernel,
        "early",
        8000000,
        out_shape=(
            held(18, YB * CX, 128),
            held(12, YB * CX, 128),
            held(54, ROWS, 128),
            held(36, ROWS, 128),
        ),
        in_specs=[HBM, VM, VM],
        out_specs=[VM] * 4,
        scratch_shapes=[dma((9,))],
    )(links, xs, ys)
    zb = shifted(zb, "zt", 1)
    zf = shifted(zf, "zt", -1)
    force = kernel_call(
        late_kernel,
        "late",
        8000000,
        out_shape=FORCE,
        in_specs=[VM] * 4,
        out_specs=HBM,
        scratch_shapes=[held(36, ROWS, 128), dma((24,))],
    )(ul, xs, ys, done)
    fx = kernel_call(
        edge_x_kernel,
        "edge_x",
        4000000,
        out_shape=held(18, ROWS, 128),
        in_specs=[VM] * 5,
        out_specs=VM,
        scratch_shapes=[held(18, YB * 8, 128)],
    )(xf, xb, ux, xs, ys)
    return kernel_call(
        edge_z_kernel,
        "edge_z",
        4000000,
        out_shape=FORCE,
        in_specs=[VM] * 6 + [HBM],
        out_specs=HBM,
        input_output_aliases={6: 0},
        scratch_shapes=[held(18, ROWS, 128), held(18, ROWS, 128), dma((12,))],
    )(zf, zb, ul, xs, ys, fx, force)


def solution(mesh):
    placed = (P(None, None, "xy", "zt", None), P(None, "xy", "zt", None), P(None, "xy", "zt", None))
    return jax.shard_map(
        per_device,
        mesh=mesh,
        in_specs=placed,
        out_specs=P(None, None, "xy", "zt", None),
        check_vma=False,
    )
```

time: 21.1 us -> 23.5 us (1.11)
  the two profiles are of different devices: /device:TPU:26 before, /device:TPU:1 now
where the time goes in v2:
time: 23.5 us; the launch traced here: 23.4 us
  Pallas kernels  9.95 us (42%)
  starting transfers between devices  7.82 us (33%)
  waiting for transfers between devices  5.54 us (24%)
    ppermute x4, starting transfers between devices, shifted(): lax.ppermute(value, axis, [(i, (i + step) % size) for i in range(size)])  7.82 us
    ppermute x4, waiting for transfers between devices, shifted(): lax.ppermute(value, axis, [(i, (i + step) % size) for i in range(size)])  5.54 us
    pallas_call x1, Pallas kernels, per_device(): kernel_call(early_kernel, 'early', 8000000, out_shape=(held(18, YB * CX,...  2.96 us
    pallas_call x1, Pallas kernels, per_device(): kernel_call(late_kernel, 'late', 8000000, out_shape=FORCE, in_specs=[VM]...  2.57 us
    pallas_call x1, Pallas kernels, per_device(): kernel_call(edge_z_kernel, 'edge_z', 4000000, out_shape=FORCE, in_specs=[...  1.89 us
    pallas_call x1, Pallas kernels, per_device(): kernel_call(prep_kernel, 'prep', 3000000, out_shape=(held(18, YB, CZ, 128...  1.58 us
    pallas_call x1, Pallas kernels, per_device(): kernel_call(edge_x_kernel, 'edge_x', 4000000, out_shape=held(18, ROWS, 12...  0.96 us
  transfers between devices with their start and end apart: 4, of which 1 were waited for; matrix products, arithmetic and copies ran while one was open for 0% of the time, Pallas kernels for 15%

profile of v2, /device:TPU:1, one launch (start us, length us, event | category | flops | bytes accessed | tf_op | source)
XLA Modules:
  0.0 23.4 jit_solution(12942416931975989059)
XLA Ops:
  0.0 1.6 %prep.1 = (f32[18,3,4,128]{3,2,1,0:T(4,128)S(1)}, f32[12,3,4,128]{3,2,1,0:T(4,128)S(1)}, f32[18,96,128]{2,1,0:T(8,128)S(1)}, f32[6,96,128]{2,1,0:T(8,128)S(1)}, f32[6,96,128]{2,1,0:T(8,128)S(1)}) custom-call(f32[4,18,8,4,384]{4,3,2,1,0:T(4,128)} %links.3, f32[6,8,4,384]{3,2,1,0:T(4,128)} %sol.1, f32[6,8,4,384]{3,2,1,0:T(4,128)} %prod.1), custom_call_target="tpu_custom_call" | custom-call | flops 3000000 | bytes 3000000 | tf_op jit(solution)/shard_map/prep/pallas_call | solution.py:380
  1.6 3.0 %early.1 = (f32[18,24,128]{2,1,0:T(8,128)S(1)}, f32[12,24,128]{2,1,0:T(8,128)S(1)}, f32[54,96,128]{2,1,0:T(8,128)S(1)}, f32[36,96,128]{2,1,0:T(8,128)S(1)}) custom-call(f32[4,18,8,4,384]{4,3,2,1,0:T(4,128)} %links.3, f32[6,96,128]{2,1,0:T(8,128)S(1)} %get-tuple-element.14.xs, f32[6,96,128]{2,1,0:T(8,128)S(1)} %get-tuple-element.15.ys), custom_call_target="tpu_custom_call" | custom-call | flops 8000000 | bytes 8000000 | tf_op jit(solution)/shard_map/early/pallas_call | solution.py:397
  4.6 4.9 %collective-permute-start = (f32[18,24,128]{2,1,0:T(8,128)S(1)}, f32[18,24,128]{2,1,0:T(8,128)S(1)}, u32[]{:S(2)}, u32[]{:S(2)}) collective-permute-start(f32[18,24,128]{2,1,0:T(8,128)S(1)} %get-tuple-element.16), channel_id=1, source_target_pairs={{0,31},{1,0},{2,1},{3,2},{4,3},{5,4},{6,5},{7,6},{8,7},{9,8},{10,9... | collective-permute-start | bytes 663560 | tf_op jit(solution)/shard_map/ppermute | solution.py:372
  9.5 0.0 collective-permute-start.1
  9.5 2.9 %collective-permute-start.2 = (f32[18,3,4,128]{3,2,1,0:T(4,128)S(1)}, f32[18,3,4,128]{3,2,1,0:T(4,128)S(1)}, u32[]{:S(2)}, u32[]{:S(2)}) collective-permute-start(f32[18,3,4,128]{3,2,1,0:T(4,128)S(1)} %get-tuple-element.19), channel_id=1, source_target_pairs={{0,224},{32,0},{64,32},{96,64},{128,96},{160,128},{192,160},{224,1... | collective-permute-start | bytes 331784 | tf_op jit(solution)/shard_map/ppermute | solution.py:372
  12.4 0.0 collective-permute-start.3
  12.4 2.6 %late.1._ = f32[4,18,8,4,384]{4,3,2,1,0:T(4,128)} custom-call(f32[54,96,128]{2,1,0:T(8,128)S(1)} %get-tuple-element.18.ul, f32[6,96,128]{2,1,0:T(8,128)S(1)} %get-tuple-element.14.xs, f32[6,96,128]{2,1,0:T(8,128)S(1)} %get-tuple-element.15.ys, f32[36,96,128]{2,1,0:T(8,128)S(1)} %get-tuple-element.22.done), custom_call_target="tpu_custom_call" | custom-call | flops 8000000 | bytes 8000000 | tf_op jit(solution)/shard_map/late/pallas_call | solution.py:413
  14.9 5.5 %collective-permute-done.3.xb = f32[12,3,4,128]{3,2,1,0:T(4,128)S(1)} collective-permute-done((f32[12,3,4,128]{3,2,1,0:T(4,128)S(1)}, f32[12,3,4,128]{3,2,1,0:T(4,128)S(1)}, u32[]{:S(2)}, u32[]{:S(2)}) %collective-permute-start.3) | collective-permute-done | bytes 73760 | tf_op jit(solution)/shard_map/ppermute | solution.py:372
  20.5 0.0 collective-permute-done.2.xf
  20.5 1.0 %edge_x.1.fx = f32[18,96,128]{2,1,0:T(8,128)S(1)} custom-call(f32[18,3,4,128]{3,2,1,0:T(4,128)S(1)} %collective-permute-done.2.xf, f32[12,3,4,128]{3,2,1,0:T(4,128)S(1)} %collective-permute-done.3.xb, f32[18,96,128]{2,1,0:T(8,128)S(1)} %get-tuple-element.21.ux, f32[6,96,128]{2,1,0:T(8,128)S(1)} %get-tuple-element.14.xs, f32[6,96,128]{2,1,0:T(8,128)S(1)} %get-tuple-element.15.ys), custom_call_target="tpu_custom_call" | custom-call | flops 4000000 | bytes 4000000 | tf_op jit(solution)/shard_map/edge_x/pallas_call | solution.py:422
  21.5 0.0 collective-permute-done.1.zb
  21.5 0.0 collective-permute-done.zf
  21.5 1.9 %edge_z.1 = f32[4,18,8,4,384]{4,3,2,1,0:T(4,128)} custom-call(f32[18,24,128]{2,1,0:T(8,128)S(1)} %collective-permute-done.zf, f32[12,24,128]{2,1,0:T(8,128)S(1)} %collective-permute-done.1.zb, f32[54,96,128]{2,1,0:T(8,128)S(1)} %get-tuple-element.18.ul, f32[6,96,128]{2,1,0:T(8,128)S(1)} %get-tuple-element.14.xs, ...), custom_call_target="tpu_custom_call", output_to_operand_aliasing={{}: (6, {})} | custom-call | flops 4000000 | bytes 4000000 | tf_op jit(solution)/shard_map/edge_z/pallas_call | solution.py:431
Async XLA Ops:
  4.6 16.9 %collective-permute-start = (f32[18,24,128]{2,1,0:T(8,128)S(1)}, f32[18,24,128]{2,1,0:T(8,128)S(1)}, u32[]{:S(2)}, u32[]{:S(2)}) collective-permute-start(f32[18,24,128]{2,1,0:T(8,128)S(1)} %get-tuple-element.16), channel_id=1, source_target_pairs={{0,31},{1,0},{2,1},{3,2},{4,3},{5,4},{6,5},{7,6},{8,7},{9,8},{10,9... | collective-permute-start | bytes 663560 | tf_op jit(solution)/shard_map/ppermute | solution.py:372
  9.5 12.0 %collective-permute-start.1 = (f32[12,24,128]{2,1,0:T(8,128)S(1)}, f32[12,24,128]{2,1,0:T(8,128)S(1)}, u32[]{:S(2)}, u32[]{:S(2)}) collective-permute-start(f32[12,24,128]{2,1,0:T(8,128)S(1)} %get-tuple-element.17), channel_id=1, source_target_pairs={{0,1},{1,2},{2,3},{3,4},{4,5},{5,6},{6,7},{7,8},{8,9},{9,10},{10,1... | collective-permute-start | bytes 442376 | tf_op jit(solution)/shard_map/ppermute | solution.py:372
  9.5 11.0 %collective-permute-start.2 = (f32[18,3,4,128]{3,2,1,0:T(4,128)S(1)}, f32[18,3,4,128]{3,2,1,0:T(4,128)S(1)}, u32[]{:S(2)}, u32[]{:S(2)}) collective-permute-start(f32[18,3,4,128]{3,2,1,0:T(4,128)S(1)} %get-tuple-element.19), channel_id=1, source_target_pairs={{0,224},{32,0},{64,32},{96,64},{128,96},{160,128},{192,160},{224,1... | collective-permute-start | bytes 331784 | tf_op jit(solution)/shard_map/ppermute | solution.py:372
  12.4 8.1 %collective-permute-start.3 = (f32[12,3,4,128]{3,2,1,0:T(4,128)S(1)}, f32[12,3,4,128]{3,2,1,0:T(4,128)S(1)}, u32[]{:S(2)}, u32[]{:S(2)}) collective-permute-start(f32[12,3,4,128]{3,2,1,0:T(4,128)S(1)} %get-tuple-element.20), channel_id=1, source_target_pairs={{0,32},{32,64},{64,96},{96,128},{128,160},{160,192},{192,224},{224... | collective-permute-start | bytes 221192 | tf_op jit(solution)/shard_map/ppermute | solution.py:372

commit v3 on v2

v3 whole, which is shorter than its diff:
```python
import jax
import jax.numpy as jnp
from jax import lax
from jax.experimental import pallas as pl
from jax.experimental.pallas import tpu as pltpu
from jax.sharding import PartitionSpec as P

NT = 24
CX, CZ, YT, YB = 8, 4, 384, 3
ROWS = YB * CX * CZ

coef_one = 9.0 / 8.0
coef_naik = -1.0 / 24.0

F32 = jnp.float32

LOCAL_COST = 1200000000
EDGE_Z_COST = 4000000


def mat_vec(u, v):
    out_r, out_i = [], []
    for a in range(3):
        re = im = None
        for b in range(3):
            ur, ui = u(3 * a + b), u(9 + 3 * a + b)
            r = ur * v[b] - ui * v[3 + b]
            i = ur * v[3 + b] + ui * v[b]
            re, im = (r, i) if re is None else (re + r, im + i)
        out_r.append(re)
        out_i.append(im)
    return out_r + out_i


def adj_vec(u, v):
    out_r, out_i = [], []
    for a in range(3):
        re = im = None
        for b in range(3):
            ur, ui = u(3 * b + a), u(9 + 3 * b + a)
            r = ur * v[b] + ui * v[3 + b]
            i = ur * v[3 + b] - ui * v[b]
            re, im = (r, i) if re is None else (re + r, im + i)
        out_r.append(re)
        out_i.append(im)
    return out_r + out_i


def store_force(put, v1, y, p1, q1, x, q2):
    for a in range(3):
        for b in range(3):
            re = im = None
            for p, q in ((v1, y), (p1, q1), (x, q2)):
                r = p[a] * q[b] + p[3 + a] * q[3 + b]
                i = p[3 + a] * q[b] - p[a] * q[3 + b]
                re, im = (r, i) if re is None else (re + r, im + i)
            put(3 * a + b, re)
            put(9 + 3 * a + b, im)


def tiles(ref):
    return ref.reshape(ref.shape[0], YB, CX, CZ, 128)


def lanes(yb):
    return pl.ds(128 * yb, 128)


class Loads:
    def __init__(self, sem):
        self.sem, self.copies, self.count = sem, {}, 0

    def start(self, name, src, dst):
        copy = pltpu.make_async_copy(src, dst, self.sem.at[self.count])
        copy.start()
        self.copies.setdefault(name, []).append(copy)
        self.count += 1

    def wait(self, name):
        for copy in self.copies.pop(name):
            copy.wait()


def vector(ref, rows, first=0):
    return [ref[first + c, rows, :] for c in range(6)]


def prep_kernel(links, sol, prod, far, near, ux, uz, xs, ys, sem):
    loads = Loads(sem)
    uxt, uzt, xst, yst = tiles(ux), tiles(uz), tiles(xs), tiles(ys)
    for yb in range(YB):
        loads.start("x", sol.at[:, :, :, lanes(yb)], xst.at[:, yb])
    for yb in range(YB):
        loads.start("uz", links.at[2, :, :, :, lanes(yb)], uzt.at[:, yb])
    for yb in range(YB):
        loads.start("y", prod.at[:, :, :, lanes(yb)], yst.at[:, yb])
    for yb in range(YB):
        loads.start("ux", links.at[0, :, :, :, lanes(yb)], uxt.at[:, yb])

    def layer(z):
        return pl.ds(z, YB * CX, stride=CZ)

    def u_z(z):
        return lambda c: uz[c, layer(z), :]

    loads.wait("x")
    loads.wait("uz")
    p1 = mat_vec(u_z(0), vector(xs, layer(1)))
    p2 = mat_vec(u_z(0), mat_vec(u_z(1), vector(xs, layer(2))))
    ahead = vector(xs, layer(0)) + p1 + p2
    loads.wait("y")
    q1 = [coef_naik * v for v in adj_vec(u_z(3), vector(ys, layer(3)))]
    q2 = adj_vec(u_z(3), [coef_naik * v for v in adj_vec(u_z(2), vector(ys, layer(2)))])
    behind = q1 + q2

    def put(to_before, to_after):
        for c, value in enumerate(ahead):
            to_before[c] = value
        for c, value in enumerate(behind):
            to_after[c] = value

    odd = lax.axis_index("zt") % 2
    pl.when(odd == 0)(lambda: put(far, near))
    pl.when(odd == 1)(lambda: put(near, far))
    loads.wait("ux")


def move_y(v, step):
    lane = lax.broadcasted_iota(jnp.int32, (8, 128), 1)
    if step > 0:
        r = [pltpu.roll(a, 128 - NT, 1) for a in v]
        return [jnp.where(lane < 128 - NT, r[k], r[(k + 1) % YB]) for k in range(YB)]
    r = [pltpu.roll(a, NT, 1) for a in v]
    return [jnp.where(lane >= NT, r[k], r[(k - 1) % YB]) for k in range(YB)]


def move_t(v, step):
    lane = lax.broadcasted_iota(jnp.int32, (8, 128), 1)
    out = []
    if step > 0:
        near = [pltpu.roll(a, 127, 1) for a in v]
        wrap = [pltpu.roll(a, NT - 1, 1) for a in v]
        for k in range(YB):
            edge = (lane + 128 * k) % NT == NT - 1
            far = wrap[k] if k == 0 else jnp.where(lane < NT - 1, wrap[k - 1], wrap[k])
            beside = near[k] if k == YB - 1 else jnp.where(lane == 127, near[k + 1], near[k])
            out.append(jnp.where(edge, far, beside))
        return out
    near = [pltpu.roll(a, 1, 1) for a in v]
    wrap = [pltpu.roll(a, 128 - (NT - 1), 1) for a in v]
    for k in range(YB):
        edge = (lane + 128 * k) % NT == 0
        far = wrap[k] if k == YB - 1 else jnp.where(lane >= 128 - (NT - 1), wrap[k + 1], wrap[k])
        beside = near[k] if k == 0 else jnp.where(lane == 0, near[k - 1], near[k])
        out.append(jnp.where(edge, far, beside))
    return out


def local_piece(d, piece, move, ul, xs, ys, fs):
    rows = [pl.ds(pl.multiple_of(yb * CX * CZ + piece * 8, 8), 8) for yb in range(YB)]

    def shift(vecs, step):
        moved = [move([vecs[k][c] for k in range(YB)], step) for c in range(6)]
        return [[moved[c][k] for c in range(6)] for k in range(YB)]

    def u(k):
        return lambda c: ul[18 * d + c, rows[k], :]

    x = shift([vector(xs, r) for r in rows], 1)
    p1 = shift([mat_vec(u(k), x[k]) for k in range(YB)], 1)
    p2 = shift([mat_vec(u(k), p1[k]) for k in range(YB)], 1)
    v1 = [[coef_one * a + coef_naik * b for a, b in zip(x[k], p2[k])] for k in range(YB)]
    y = [vector(ys, r) for r in rows]
    q1 = [adj_vec(u(k), y[k]) for k in range(YB)]
    q1 = shift([[coef_naik * a for a in v] for v in q1], -1)
    q2 = shift([adj_vec(u(k), q1[k]) for k in range(YB)], -1)
    for k in range(YB):

        def put(c, value, k=k):
            fs[18 * d + c, rows[k], :] = value

        store_force(put, v1[k], y[k], p1[k], q1[k], x[k], q2[k])


def load_local(loads, links, ul):
    for d, mu in enumerate((1, 3)):
        for yb in range(YB):
            src, dst = links.at[mu, :, :, :, lanes(yb)], tiles(ul).at[pl.ds(18 * d, 18), yb]
            loads.start(mu, src, dst)


def local_pieces(d, first, end, ul, xs, ys, fs, sent=None):
    def body(piece, carry):
        local_piece(d, piece, (move_y, move_t)[d], ul, xs, ys, fs)
        if sent is not None:
            sent(piece)
        return carry

    lax.fori_loop(first, end, body, 0)


def first_products(ux, uz, xs, ys, pre):
    def body_z(piece, carry):
        rows = pl.ds(pl.multiple_of(piece * 8, 8), 8)
        x = [pltpu.roll(a, 7, 0) for a in vector(xs, rows)]
        y = vector(ys, rows)
        p1 = mat_vec(lambda c: uz[c, rows, :], x)
        w1 = adj_vec(lambda c: uz[c, rows, :], y)
        wx = adj_vec(lambda c: ux[c, rows, :], y)
        for c in range(6):
            pre[c, rows, :] = p1[c]
            pre[6 + c, rows, :] = coef_naik * w1[c]
            pre[18 + c, rows, :] = coef_naik * wx[c]
        return carry

    lax.fori_loop(0, ROWS // 8, body_z, 0)
    low = lax.broadcasted_iota(jnp.int32, (8, 128), 0) < CZ

    def body_x(yb, carry):
        rows = [pl.ds(pl.multiple_of(yb * CX * CZ + k * 8, 8), 8) for k in range(4)]
        half = [[pltpu.roll(a, CZ, 0) for a in vector(xs, r)] for r in rows]
        for k in range(3):
            x = [jnp.where(low, a, b) for a, b in zip(half[k], half[k + 1])]
            for c, value in enumerate(mat_vec(lambda c: ux[c, rows[k], :], x)):
                pre[12 + c, rows[k], :] = value
        return carry

    lax.fori_loop(0, YB, body_x, 0)


def early_kernel(links, ux, uz, xs, ys, _, far, xf, xb, ul, fs, pre, sem):
    def u_x(row):
        return lambda c: ux[c, pl.ds(row, 8), :]

    for yb in range(YB):
        last = yb * CX * CZ + (CX - 2) * CZ
        w1 = [coef_naik * v for v in adj_vec(u_x(last), vector(ys, pl.ds(last, 8)))]
        w2 = adj_vec(u_x(last), [pltpu.roll(v, 4, 0) for v in w1])
        for c, value in enumerate(w1 + w2):
            xb[c, yb] = value[CZ:]
        base = yb * CX * CZ
        p1 = mat_vec(u_x(base), vector(xs, pl.ds(base + CZ, 8)))
        p2 = mat_vec(u_x(base), [pltpu.roll(v, 4, 0) for v in p1])
        for c, value in enumerate(vector(xs, pl.ds(base, 8)) + p1 + p2):
            xf[c, yb] = value[:CZ]

    @pl.when(lax.axis_index("zt") == 0)
    def _():
        loads = Loads(sem)
        load_local(loads, links, ul)
        first_products(ux, uz, xs, ys, pre)
        for d, mu in enumerate((1, 3)):
            loads.wait(mu)
            local_pieces(d, 0, 4, ul, xs, ys, fs)


def local_kernel(links, ux, uz, xs, ys, _, __, ___, ul, fs, pre, force, sem, sem_out):
    first = lax.axis_index("zt") == 0
    fst = tiles(fs)

    def out_copy(piece, yb):
        return pltpu.make_async_copy(
            fst.at[pl.ds(0, 18), yb, pl.ds(2 * piece, 2)],
            force.at[1, :, pl.ds(2 * piece, 2), :, lanes(yb)],
            sem_out.at[yb * 4 + piece],
        )

    def sent(piece):
        for yb in range(YB):
            out_copy(piece, yb).start()

    @pl.when(first)
    def _():
        for piece in range(4):
            sent(piece)

    @pl.when(jnp.logical_not(first))
    def _():
        loads = Loads(sem)
        load_local(loads, links, ul)
        first_products(ux, uz, xs, ys, pre)
        loads.wait(1)
        local_pieces(0, 0, 4, ul, xs, ys, fs, sent)
        loads.wait(3)
        local_pieces(1, 0, 4, ul, xs, ys, fs)

    for yb in range(YB):
        for piece in range(4):
            out_copy(piece, yb).wait()


def edge_x_kernel(xf, xb, ux, xs, ys, pre, fz, _, force, fx, hx, sem):
    def out_copy(src, mu, yb):
        return pltpu.make_async_copy(
            tiles(src).at[:, yb], force.at[mu, :, :, :, lanes(yb)], sem.at[mu // 2 * YB + yb]
        )

    for yb in range(YB):
        out_copy(fz, 2, yb).start()
    low = lax.broadcasted_iota(jnp.int32, (8, 128), 0) < CZ
    for yb in range(YB):
        for c in range(18):
            hx[c, pl.ds(yb * 8 + CZ, CZ), :] = xf[c, yb]
        for c in range(12):
            hx[c, pl.ds(yb * 8, CZ), :] = xb[c, yb]

    def body(yb, carry):
        rows = [pl.ds(pl.multiple_of(yb * CX * CZ + k * 8, 8), 8) for k in range(4)]
        edge = pl.ds(pl.multiple_of(yb * 8, 8), 8)

        def half(vecs):
            return [[pltpu.roll(a, CZ, 0) for a in v] for v in vecs]

        def joined(r):
            return [[jnp.where(low, a, b) for a, b in zip(r[k], r[k + 1])] for k in range(4)]

        def ahead(vecs, first):
            return joined(half(vecs) + [vector(hx, edge, first)])

        def back(vecs, first):
            return joined([vector(hx, edge, first)] + half(vecs))

        def u(k):
            return lambda c: ux[c, rows[k], :]

        x = ahead([vector(xs, r) for r in rows], 0)
        p1 = ahead([vector(pre, r, 12) for r in rows[:3]] + [mat_vec(u(3), x[3])], 6)
        p2 = ahead([mat_vec(u(k), p1[k]) for k in range(4)], 12)
        v1 = [[coef_one * a + coef_naik * b for a, b in zip(x[k], p2[k])] for k in range(4)]
        y = [vector(ys, r) for r in rows]
        q1 = back([vector(pre, r, 18) for r in rows], 0)
        q2 = back([adj_vec(u(k), q1[k]) for k in range(4)], 6)
        for k in range(4):

            def put(c, value, k=k):
                fx[c, rows[k], :] = value

            store_force(put, v1[k], y[k], p1[k], q1[k], x[k], q2[k])
        out_copy(fx, 0, yb).start()
        return carry

    lax.fori_loop(0, YB, body, 0)
    for yb in range(YB):
        out_copy(fz, 2, yb).wait()
        out_copy(fx, 0, yb).wait()


def edge_z_kernel(far, near, ul, xs, ys, pre, fs, _, fz, force, hz, sem):
    def out_t(yb):
        return pltpu.make_async_copy(
            tiles(fs).at[pl.ds(18, 18), yb], force.at[3, :, :, :, lanes(yb)], sem.at[yb]
        )

    for yb in range(YB):
        out_t(yb).start()
    top_rows = pl.ds(CZ - 1, YB * CX, stride=CZ)

    def spread(zf, zb):
        p1 = mat_vec(lambda c: ul[c, top_rows, :], [zf[c] for c in range(6)])
        for c, value in enumerate([zf[c] for c in range(18)] + p1):
            hz[c, top_rows, :] = value
        for c in range(12):
            hz[c, pl.ds(0, YB * CX, stride=CZ), :] = zb[c]

    odd = lax.axis_index("zt") % 2
    pl.when(odd == 0)(lambda: spread(near, far))
    pl.when(odd == 1)(lambda: spread(far, near))
    row = lax.broadcasted_iota(jnp.int32, (8, 128), 0)
    top, bottom = row % CZ == CZ - 1, row % CZ == 0

    def body(piece, yb):
        rows = pl.ds(pl.multiple_of(yb * CX * CZ + piece * 8, 8), 8)

        def ahead(v, first):
            halo = vector(hz, rows, first)
            return [jnp.where(top, h, pltpu.roll(a, 7, 0)) for a, h in zip(v, halo)]

        def back(v, first):
            halo = vector(hz, rows, first)
            return [jnp.where(bottom, h, pltpu.roll(a, 1, 0)) for a, h in zip(v, halo)]

        def u(c):
            return ul[c, rows, :]

        x = ahead(vector(xs, rows), 0)
        own = [jnp.where(top, h, a) for a, h in zip(vector(pre, rows), vector(hz, rows, 18))]
        p1 = ahead(own, 6)
        p2 = ahead(mat_vec(u, p1), 12)
        v1 = [coef_one * a + coef_naik * b for a, b in zip(x, p2)]
        y = vector(ys, rows)
        q1 = back(vector(pre, rows, 6), 0)
        q2 = back(adj_vec(u, q1), 6)

        def put(c, value):
            fz[c, rows, :] = value

        store_force(put, v1, y, p1, q1, x, q2)
        return yb

    for yb in range(YB):
        lax.fori_loop(0, 4, body, yb)
    for yb in range(YB):
        out_t(yb).wait()


HBM = pl.BlockSpec(memory_space=pltpu.HBM)
VM = pl.BlockSpec(memory_space=pltpu.VMEM)
FORCE = jax.ShapeDtypeStruct((4, 18, CX, CZ, YT), F32)


def held(*shape):
    return pltpu.VMEM(shape, F32)


def kernel_call(body, name, flops, **args):
    return pl.pallas_call(
        body,
        name=name,
        cost_estimate=pl.CostEstimate(flops=flops, bytes_accessed=flops, transcendentals=0),
        compiler_params=pltpu.CompilerParams(vmem_limit_bytes=16 << 20),
        **args,
    )


def shifted(value, axis, step):
    size = lax.axis_size(axis)
    return lax.ppermute(value, axis, [(i, (i + step) % size) for i in range(size)])


def per_device(links, solution, product):
    links, solution, product = (
        pltpu.with_memory_space_constraint(a, pltpu.HBM) for a in (links, solution, product)
    )
    dma = pltpu.SemaphoreType.DMA
    far, near, ux, uz, xs, ys = kernel_call(
        prep_kernel,
        "prep",
        3000000,
        out_shape=(
            held(18, YB * CX, 128),
            held(20, YB * CX, 128),
            held(18, ROWS, 128),
            held(18, ROWS, 128),
            held(6, ROWS, 128),
            held(6, ROWS, 128),
        ),
        in_specs=[HBM] * 3,
        out_specs=[VM] * 6,
        scratch_shapes=[dma((12,))],
    )(links, solution, product)
    size = lax.axis_size("zt")
    near = lax.ppermute(near, "zt", [(i, i ^ 1) for i in range(size)])
    far, xf, xb, ul, fs, pre = kernel_call(
        early_kernel,
        "early",
        1000000,
        out_shape=(
            held(18, YB * CX, 128),
            held(18, YB, CZ, 128),
            held(12, YB, CZ, 128),
            held(36, ROWS, 128),
            held(36, ROWS, 128),
            held(24, ROWS, 128),
        ),
        in_specs=[HBM] + [VM] * 5,
        out_specs=[VM] * 6,
        input_output_aliases={5: 0},
        scratch_shapes=[dma((6,))],
    )(links, ux, uz, xs, ys, far)
    far = lax.ppermute(far, "zt", [(i, (i + 2 * (i % 2) - 1) % size) for i in range(size)])
    xb = shifted(xb, "xy", 1)
    xf = shifted(xf, "xy", -1)
    _, fs, pre, force = kernel_call(
        local_kernel,
        "local",
        LOCAL_COST,
        out_shape=(held(36, ROWS, 128), held(36, ROWS, 128), held(24, ROWS, 128), FORCE),
        in_specs=[HBM] + [VM] * 7,
        out_specs=[VM, VM, VM, HBM],
        input_output_aliases={5: 0, 6: 1, 7: 2},
        scratch_shapes=[dma((6,)), dma((12,))],
    )(links, ux, uz, xs, ys, ul, fs, pre)
    fz, force = kernel_call(
        edge_z_kernel,
        "edge_z",
        EDGE_Z_COST,
        out_shape=(held(18, ROWS, 128), FORCE),
        in_specs=[VM] * 7 + [HBM],
        out_specs=[VM, HBM],
        input_output_aliases={7: 1},
        scratch_shapes=[held(24, ROWS, 128), dma((3,))],
    )(far, near, uz, xs, ys, pre, fs, force)
    return kernel_call(
        edge_x_kernel,
        "edge_x",
        4000000,
        out_shape=FORCE,
        in_specs=[VM] * 7 + [HBM],
        out_specs=HBM,
        input_output_aliases={7: 0},
        scratch_shapes=[held(18, ROWS, 128), held(18, YB * 8, 128), dma((6,))],
    )(xf, xb, ux, xs, ys, pre, fz, force)


def solution(mesh):
    placed = (P(None, None, "xy", "zt", None), P(None, "xy", "zt", None), P(None, "xy", "zt", None))
    return jax.shard_map(
        per_device,
        mesh=mesh,
        in_specs=placed,
        out_specs=P(None, None, "xy", "zt", None),
        check_vma=False,
    )
```

time: 23.5 us -> 19.4 us (0.83)
  the two profiles are of different devices: /device:TPU:1 before, /device:TPU:26 now
where the time goes in v3:
time: 19.4 us; the launch traced here: 19.1 us
  Pallas kernels  9.76 us (50%)
  starting transfers between devices  5.48 us (28%)
  waiting for transfers between devices  3.85 us (20%)
    pallas_call x1, Pallas kernels, per_device(): kernel_call(early_kernel, 'early', 1000000, out_shape=(held(18, YB * CX,...  4.41 us
    ppermute x1, starting transfers between devices, per_device(): lax.ppermute(far, 'zt', [(i, (i + 2 * (i % 2) - 1) % size) for i in range...  3.37 us
    ppermute x1, waiting for transfers between devices, per_device(): lax.ppermute(far, 'zt', [(i, (i + 2 * (i % 2) - 1) % size) for i in range...  2.7 us
    ppermute x2, starting transfers between devices, shifted(): lax.ppermute(value, axis, [(i, (i + step) % size) for i in range(size)])  2.03 us
    pallas_call x1, Pallas kernels, per_device(): kernel_call(prep_kernel, 'prep', 3000000, out_shape=(held(18, YB * CX, 12...  1.75 us
    pallas_call x1, Pallas kernels, per_device(): kernel_call(edge_x_kernel, 'edge_x', 4000000, out_shape=FORCE, in_specs=[...  1.55 us
    ppermute x2, waiting for transfers between devices, shifted(): lax.ppermute(value, axis, [(i, (i + step) % size) for i in range(size)])  1.14 us
    pallas_call x1, Pallas kernels, per_device(): kernel_call(local_kernel, 'local', LOCAL_COST, out_shape=(held(36, ROWS,...  1.06 us
  transfers between devices with their start and end apart: 4, of which 2 were waited for; matrix products, arithmetic and copies ran while one was open for 0% of the time, Pallas kernels for 34%

profile of v3, /device:TPU:26, one launch (start us, length us, event | category | flops | bytes accessed | tf_op | source)
XLA Modules:
  0.0 19.1 jit_solution(11146597290045680038)
XLA Ops:
  0.0 1.7 %prep.1 = (f32[18,24,128]{2,1,0:T(8,128)S(1)}, f32[20,24,128]{2,1,0:T(8,128)S(1)}, f32[18,96,128]{2,1,0:T(8,128)S(1)}, f32[18,96,128]{2,1,0:T(8,128)S(1)}, f32[6...) custom-call(f32[4,18,8,4,384]{4,3,2,1,0:T(4,128)} %links.5, f32[6,8,4,384]{3,2,1,0:T(4,128)} %sol.1, f32[6,8,4,384]{3,2,1,0:T(4,128)} %prod.1), custom_call_target="tpu_custom_call" | custom-call | flops 3000000 | bytes 3000000 | tf_op jit(solution)/shard_map/prep/pallas_call | solution.py:435
  1.8 0.1 collective-permute-start.3
  1.9 4.4 %early.1 = (f32[18,24,128]{2,1,0:T(8,128)S(1)}, f32[18,3,4,128]{3,2,1,0:T(4,128)S(1)}, f32[12,3,4,128]{3,2,1,0:T(4,128)S(1)}, f32[36,96,128]{2,1,0:T(8,128)S(1)}...) custom-call(f32[4,18,8,4,384]{4,3,2,1,0:T(4,128)} %links.5, ...), custom_call_target="tpu_custom_call", output_to_operand_aliasing={{0}: (5, {})} | custom-call | flops 1000000 | bytes 1000000 | tf_op jit(solution)/shard_map/early/pallas_call | solution.py:453
  6.3 3.4 %collective-permute-start.2 = (f32[18,24,128]{2,1,0:T(8,128)S(1)}, f32[18,24,128]{2,1,0:T(8,128)S(1)}, u32[]{:S(2)}, u32[]{:S(2)}) collective-permute-start(f32[18,24,128]{2,1,0:T(8,128)S(1)} %get-tuple-element.33), channel_id=1, source_target_pairs={{0,31},{1,2},{2,1},{3,4},{4,3},{5,6},{6,5},{7,8},{8,7},{9,10},{10,... | collective-permute-start | bytes 663560 | tf_op jit(solution)/shard_map/ppermute | solution.py:470
  9.6 1.1 %collective-permute-start.1 = (f32[12,3,4,128]{3,2,1,0:T(4,128)S(1)}, f32[12,3,4,128]{3,2,1,0:T(4,128)S(1)}, u32[]{:S(2)}, u32[]{:S(2)}) collective-permute-start(f32[12,3,4,128]{3,2,1,0:T(4,128)S(1)} %get-tuple-element.28), channel_id=1, source_target_pairs={{0,32},{32,64},{64,96},{96,128},{128,160},{160,192},{192,224},{224... | collective-permute-start | bytes 221192 | tf_op jit(solution)/shard_map/ppermute | solution.py:427
  10.7 0.9 %collective-permute-start = (f32[18,3,4,128]{3,2,1,0:T(4,128)S(1)}, f32[18,3,4,128]{3,2,1,0:T(4,128)S(1)}, u32[]{:S(2)}, u32[]{:S(2)}) collective-permute-start(f32[18,3,4,128]{3,2,1,0:T(4,128)S(1)} %get-tuple-element.27), channel_id=1, source_target_pairs={{0,224},{32,0},{64,32},{96,64},{128,96},{160,128},{192,160},{224,1... | collective-permute-start | bytes 331784 | tf_op jit(solution)/shard_map/ppermute | solution.py:427
  11.7 1.1 %local.1 = (f32[36,96,128]{2,1,0:T(8,128)S(1)}, f32[36,96,128]{2,1,0:T(8,128)S(1)}, f32[24,96,128]{2,1,0:T(8,128)S(1)}, f32[4,18,8,4,384]{4,3,2,1,0:T(4,128)}) custom-call(f32[4,18,8,4,384]{4,3,2,1,0:T(4,128)} %links.5, f32[18,96,128]{2,1,0:T(8,128)S(1)} %get-tuple-element.22.ux, ...), custom_call_target="tpu_custom_call", output_to_operand_aliasing={{0}: (5, {}), {1}: (6, {}), {2}: (7, {})} | custom-call | flops 1200000000 | bytes 1200000000 | tf_op jit(solution)/shard_map/local/pallas_call | solution.py:473
  12.7 2.7 %collective-permute-done.2.far = f32[18,24,128]{2,1,0:T(8,128)S(1)} collective-permute-done((f32[18,24,128]{2,1,0:T(8,128)S(1)}, f32[18,24,128]{2,1,0:T(8,128)S(1)}, u32[]{:S(2)}, u32[]{:S(2)}) %collective-permute-start.2) | collective-permute-done | bytes 221216 | tf_op jit(solution)/shard_map/ppermute | solution.py:470
  15.4 0.0 collective-permute-done.3.near
  15.4 1.0 %edge_z.1 = (f32[18,96,128]{2,1,0:T(8,128)S(1)}, f32[4,18,8,4,384]{4,3,2,1,0:T(4,128)}) custom-call(f32[18,24,128]{2,1,0:T(8,128)S(1)} %collective-permute-done.2.far, f32[20,24,128]{2,1,0:T(8,128)S(1)} %collective-permute-done.3.near, f32[18,96,128]{2,1,0:T(8,128)S(1)} %get-tuple-element.23.uz.ul, ...), custom_call_target="tpu_custom_call", output_to_operand_aliasing={{1}: (7, {})} | custom-call | flops 4000000 | bytes 4000000 | tf_op jit(solution)/shard_map/edge_z/pallas_call | solution.py:483
  16.4 0.0 collective-permute-done.1.xb
  16.5 1.1 %collective-permute-done.xf = f32[18,3,4,128]{3,2,1,0:T(4,128)S(1)} collective-permute-done((f32[18,3,4,128]{3,2,1,0:T(4,128)S(1)}, f32[18,3,4,128]{3,2,1,0:T(4,128)S(1)}, u32[]{:S(2)}, u32[]{:S(2)}) %collective-permute-start) | collective-permute-done | bytes 110624 | tf_op jit(solution)/shard_map/ppermute | solution.py:427
  17.6 1.6 %edge_x.1 = f32[4,18,8,4,384]{4,3,2,1,0:T(4,128)} custom-call(f32[18,3,4,128]{3,2,1,0:T(4,128)S(1)} %collective-permute-done.xf, f32[12,3,4,128]{3,2,1,0:T(4,128)S(1)} %collective-permute-done.1.xb, f32[18,96,128]{2,1,0:T(8,128)S(1)} %get-tuple-element.22.ux, f32[6,96,128]{2,1,0:T(8,128)S(1)} %get-tuple-element.24.xs, ...), custom_call_target="tpu_custom_call", output_to_operand_aliasing={{}: (7, {})} | custom-call | flops 4000000 | bytes 4000000 | tf_op jit(solution)/shard_map/edge_x/pallas_call | solution.py:493
Async XLA Ops:
  1.8 13.7 %collective-permute-start.3 = (f32[20,24,128]{2,1,0:T(8,128)S(1)}, f32[20,24,128]{2,1,0:T(8,128)S(1)}, u32[]{:S(2)}, u32[]{:S(2)}) collective-permute-start(f32[20,24,128]{2,1,0:T(8,128)S(1)} %get-tuple-element.34), channel_id=1, source_target_pairs={{0,1},{1,0},{2,3},{3,2},{4,5},{5,4},{6,7},{7,6},{8,9},{9,8},{10,11... | collective-permute-start | bytes 737288 | tf_op jit(solution)/shard_map/ppermute | solution.py:452
  6.3 9.2 %collective-permute-start.2 = (f32[18,24,128]{2,1,0:T(8,128)S(1)}, f32[18,24,128]{2,1,0:T(8,128)S(1)}, u32[]{:S(2)}, u32[]{:S(2)}) collective-permute-start(f32[18,24,128]{2,1,0:T(8,128)S(1)} %get-tuple-element.33), channel_id=1, source_target_pairs={{0,31},{1,2},{2,1},{3,4},{4,3},{5,6},{6,5},{7,8},{8,7},{9,10},{10,... | collective-permute-start | bytes 663560 | tf_op jit(solution)/shard_map/ppermute | solution.py:470
  9.6 6.8 %collective-permute-start.1 = (f32[12,3,4,128]{3,2,1,0:T(4,128)S(1)}, f32[12,3,4,128]{3,2,1,0:T(4,128)S(1)}, u32[]{:S(2)}, u32[]{:S(2)}) collective-permute-start(f32[12,3,4,128]{3,2,1,0:T(4,128)S(1)} %get-tuple-element.28), channel_id=1, source_target_pairs={{0,32},{32,64},{64,96},{96,128},{128,160},{160,192},{192,224},{224... | collective-permute-start | bytes 221192 | tf_op jit(solution)/shard_map/ppermute | solution.py:427
  10.7 6.9 %collective-permute-start = (f32[18,3,4,128]{3,2,1,0:T(4,128)S(1)}, f32[18,3,4,128]{3,2,1,0:T(4,128)S(1)}, u32[]{:S(2)}, u32[]{:S(2)}) collective-permute-start(f32[18,3,4,128]{3,2,1,0:T(4,128)S(1)} %get-tuple-element.27), channel_id=1, source_target_pairs={{0,224},{32,0},{64,32},{96,64},{128,96},{160,128},{192,160},{224,1... | collective-permute-start | bytes 331784 | tf_op jit(solution)/shard_map/ppermute | solution.py:427

commit v4 on v3

--- a/solution.py
+++ b/solution.py
@@ -16,6 +16,8 @@
 
 LOCAL_COST = 1200000000
 EDGE_Z_COST = 4000000
+
+AHEAD = (4, 1)
 
 
 def mat_vec(u, v):
@@ -94,8 +96,10 @@
         loads.start("uz", links.at[2, :, :, :, lanes(yb)], uzt.at[:, yb])
     for yb in range(YB):
         loads.start("y", prod.at[:, :, :, lanes(yb)], yst.at[:, yb])
-    for yb in range(YB):
-        loads.start("ux", links.at[0, :, :, :, lanes(yb)], uxt.at[:, yb])
+    for first in (0, CX - 2):
+        for yb in range(YB):
+            src = links.at[0, :, pl.ds(first, 2), :, lanes(yb)]
+            loads.start("ux", src, uxt.at[:, yb, pl.ds(first, 2)])
 
     def layer(z):
         return pl.ds(z, YB * CX, stride=CZ)
@@ -182,7 +186,10 @@
         store_force(put, v1[k], y[k], p1[k], q1[k], x[k], q2[k])
 
 
-def load_local(loads, links, ul):
+def load_local(loads, links, ux, ul):
+    for yb in range(YB):
+        src = links.at[0, :, pl.ds(2, CX - 4), :, lanes(yb)]
+        loads.start(0, src, tiles(ux).at[:, yb, pl.ds(2, CX - 4)])
     for d, mu in enumerate((1, 3)):
         for yb in range(YB):
             src, dst = links.at[mu, :, :, :, lanes(yb)], tiles(ul).at[pl.ds(18 * d, 18), yb]
@@ -199,36 +206,76 @@
     lax.fori_loop(first, end, body, 0)
 
 
-def first_products(ux, uz, xs, ys, pre):
+def slices(yb):
+    return [pl.ds(pl.multiple_of(yb * CX * CZ + k * 8, 8), 8) for k in range(4)]
+
+
+def halves(vec):
+    return [pltpu.roll(a, CZ, 0) for a in vec]
+
+
+def joined(first, second):
+    low = lax.broadcasted_iota(jnp.int32, (8, 128), 0) < CZ
+    return [jnp.where(low, a, b) for a, b in zip(first, second)]
+
+
+def scaled(vec):
+    return [coef_naik * a for a in vec]
+
+
+def mixed(x, p2):
+    return [coef_one * a + coef_naik * b for a, b in zip(x, p2)]
+
+
+def first_products(loads, ux, uz, xs, ys, pre, fx):
     def body_z(piece, carry):
         rows = pl.ds(pl.multiple_of(piece * 8, 8), 8)
-        x = [pltpu.roll(a, 7, 0) for a in vector(xs, rows)]
-        y = vector(ys, rows)
-        p1 = mat_vec(lambda c: uz[c, rows, :], x)
-        w1 = adj_vec(lambda c: uz[c, rows, :], y)
-        wx = adj_vec(lambda c: ux[c, rows, :], y)
-        for c in range(6):
-            pre[c, rows, :] = p1[c]
-            pre[6 + c, rows, :] = coef_naik * w1[c]
-            pre[18 + c, rows, :] = coef_naik * wx[c]
+        p1 = mat_vec(lambda c: uz[c, rows, :], [pltpu.roll(a, 7, 0) for a in vector(xs, rows)])
+        w1 = scaled(adj_vec(lambda c: uz[c, rows, :], vector(ys, rows)))
+        for c, value in enumerate(p1 + w1):
+            pre[c, rows, :] = value
         return carry
 
     lax.fori_loop(0, ROWS // 8, body_z, 0)
-    low = lax.broadcasted_iota(jnp.int32, (8, 128), 0) < CZ
+    loads.wait(0)
 
     def body_x(yb, carry):
-        rows = [pl.ds(pl.multiple_of(yb * CX * CZ + k * 8, 8), 8) for k in range(4)]
-        half = [[pltpu.roll(a, CZ, 0) for a in vector(xs, r)] for r in rows]
-        for k in range(3):
-            x = [jnp.where(low, a, b) for a, b in zip(half[k], half[k + 1])]
-            for c, value in enumerate(mat_vec(lambda c: ux[c, rows[k], :], x)):
+        rows = slices(yb)
+
+        def u(k):
+            return lambda c: ux[c, rows[k], :]
+
+        def keep(k, vecs):
+            for c, value in enumerate(sum(vecs, [])):
                 pre[12 + c, rows[k], :] = value
+
+        y = [vector(ys, r) for r in rows]
+        h = [halves(vector(xs, r)) for r in rows]
+        x = [joined(h[k], h[k + 1]) for k in range(3)]
+        p1_raw = [mat_vec(u(k), x[k]) for k in range(3)]
+        h = [halves(v) for v in p1_raw]
+        p1 = [joined(h[0], h[1]), joined(h[1], h[2]), h[2]]
+        h = [halves(mat_vec(u(k), p1[k])) for k in range(3)]
+        v1 = [mixed(x[k], joined(h[k], h[k + 1])) for k in range(2)]
+        w1 = [scaled(adj_vec(u(k), y[k])) for k in range(4)]
+        h = [halves(v) for v in w1]
+        q1 = [h[0]] + [joined(h[k - 1], h[k]) for k in (1, 2, 3)]
+        h = [halves(adj_vec(u(k), q1[k])) for k in range(4)]
+        q2 = [None] + [joined(h[k - 1], h[k]) for k in (1, 2, 3)]
+        keep(0, [v1[0], p1[0], x[0], w1[0]])
+        keep(2, [q1[2], q2[2], p1_raw[2]])
+        keep(3, [q1[3], q2[3]])
+
+        def put(c, value):
+            fx[c, rows[1], :] = value
+
+        store_force(put, v1[1], y[1], p1[1], q1[1], x[1], q2[1])
         return carry
 
     lax.fori_loop(0, YB, body_x, 0)
 
 
-def early_kernel(links, ux, uz, xs, ys, _, far, xf, xb, ul, fs, pre, sem):
+def early_kernel(links, uz, xs, ys, _, __, far, ux, xf, xb, ul, fs, pre, fx, sem):
     def u_x(row):
         return lambda c: ux[c, pl.ds(row, 8), :]
 
@@ -247,14 +294,15 @@
     @pl.when(lax.axis_index("zt") == 0)
     def _():
         loads = Loads(sem)
-        load_local(loads, links, ul)
-        first_products(ux, uz, xs, ys, pre)
+        load_local(loads, links, ux, ul)
+        first_products(loads, ux, uz, xs, ys, pre, fx)
         for d, mu in enumerate((1, 3)):
             loads.wait(mu)
-            local_pieces(d, 0, 4, ul, xs, ys, fs)
-
-
-def local_kernel(links, ux, uz, xs, ys, _, __, ___, ul, fs, pre, force, sem, sem_out):
+            local_pieces(d, 0, AHEAD[d], ul, xs, ys, fs)
+
+
+def local_kernel(links, uz, xs, ys, *refs):
+    ux, ul, fs, pre, fx, force, sem, sem_out = refs[5:]
     first = lax.axis_index("zt") == 0
     fst = tiles(fs)
 
@@ -271,14 +319,16 @@
 
     @pl.when(first)
     def _():
-        for piece in range(4):
+        for piece in range(AHEAD[0]):
             sent(piece)
+        local_pieces(0, AHEAD[0], 4, ul, xs, ys, fs, sent)
+        local_pieces(1, AHEAD[1], 4, ul, xs, ys, fs)
 
     @pl.when(jnp.logical_not(first))
     def _():
         loads = Loads(sem)
-        load_local(loads, links, ul)
-        first_products(ux, uz, xs, ys, pre)
+        load_local(loads, links, ux, ul)
+        first_products(loads, ux, uz, xs, ys, pre, fx)
         loads.wait(1)
         local_pieces(0, 0, 4, ul, xs, ys, fs, sent)
         loads.wait(3)
@@ -289,66 +339,72 @@
             out_copy(piece, yb).wait()
 
 
-def edge_x_kernel(xf, xb, ux, xs, ys, pre, fz, _, force, fx, hx, sem):
-    def out_copy(src, mu, yb):
+def edge_back_kernel(xb, ux, ys, pre, _, __, fx, force, hx):
+    for yb in range(YB):
+        for c in range(12):
+            hx[c, pl.ds(yb * 8, CZ), :] = xb[c, yb]
+    for yb in range(YB):
+        rows = slices(yb)[0]
+        edge = pl.ds(yb * 8, 8)
+        q1 = joined(vector(hx, edge), halves(vector(pre, rows, 30)))
+        w2 = adj_vec(lambda c: ux[c, rows, :], q1)
+        q2 = joined(vector(hx, edge, 6), halves(w2))
+
+        def put(c, value):
+            fx[c, rows, :] = value
+
+        v1, p1, x = (vector(pre, rows, first) for first in (12, 18, 24))
+        store_force(put, v1, vector(ys, rows), p1, q1, x, q2)
+
+
+def edge_ahead_kernel(xf, ux, xs, ys, pre, fx, _, force, f2, hx, sem):
+    def out_copy(src, first, yb):
         return pltpu.make_async_copy(
-            tiles(src).at[:, yb], force.at[mu, :, :, :, lanes(yb)], sem.at[mu // 2 * YB + yb]
+            tiles(src).at[:, yb, pl.ds(first, CX // 2)],
+            force.at[0, :, pl.ds(first, CX // 2), :, lanes(yb)],
+            sem.at[first // 4 * YB + yb],
         )
 
     for yb in range(YB):
-        out_copy(fz, 2, yb).start()
-    low = lax.broadcasted_iota(jnp.int32, (8, 128), 0) < CZ
-    for yb in range(YB):
+        out_copy(fx, 0, yb).start()
         for c in range(18):
             hx[c, pl.ds(yb * 8 + CZ, CZ), :] = xf[c, yb]
-        for c in range(12):
-            hx[c, pl.ds(yb * 8, CZ), :] = xb[c, yb]
-
-    def body(yb, carry):
-        rows = [pl.ds(pl.multiple_of(yb * CX * CZ + k * 8, 8), 8) for k in range(4)]
-        edge = pl.ds(pl.multiple_of(yb * 8, 8), 8)
-
-        def half(vecs):
-            return [[pltpu.roll(a, CZ, 0) for a in v] for v in vecs]
-
-        def joined(r):
-            return [[jnp.where(low, a, b) for a, b in zip(r[k], r[k + 1])] for k in range(4)]
-
-        def ahead(vecs, first):
-            return joined(half(vecs) + [vector(hx, edge, first)])
-
-        def back(vecs, first):
-            return joined([vector(hx, edge, first)] + half(vecs))
+    for yb in range(YB):
+        rows = slices(yb)
+        edge = pl.ds(yb * 8, 8)
 
         def u(k):
             return lambda c: ux[c, rows[k], :]
 
-        x = ahead([vector(xs, r) for r in rows], 0)
-        p1 = ahead([vector(pre, r, 12) for r in rows[:3]] + [mat_vec(u(3), x[3])], 6)
-        p2 = ahead([mat_vec(u(k), p1[k]) for k in range(4)], 12)
-        v1 = [[coef_one * a + coef_naik * b for a, b in zip(x[k], p2[k])] for k in range(4)]
-        y = [vector(ys, r) for r in rows]
-        q1 = back([vector(pre, r, 18) for r in rows], 0)
-        q2 = back([adj_vec(u(k), q1[k]) for k in range(4)], 6)
-        for k in range(4):
+        def ahead(second, third, first):
+            h = [halves(second), halves(third), vector(hx, edge, first)]
+            return {2: joined(h[0], h[1]), 3: joined(h[1], h[2])}
+
+        x = ahead(vector(xs, rows[2]), vector(xs, rows[3]), 0)
+        p1 = ahead(vector(pre, rows[2], 24), mat_vec(u(3), x[3]), 6)
+        p2 = ahead(mat_vec(u(2), p1[2]), mat_vec(u(3), p1[3]), 12)
+        for k in (2, 3):
 
             def put(c, value, k=k):
-                fx[c, rows[k], :] = value
-
-            store_force(put, v1[k], y[k], p1[k], q1[k], x[k], q2[k])
-        out_copy(fx, 0, yb).start()
-        return carry
-
-    lax.fori_loop(0, YB, body, 0)
-    for yb in range(YB):
-        out_copy(fz, 2, yb).wait()
-        out_copy(fx, 0, yb).wait()
-
-
-def edge_z_kernel(far, near, ul, xs, ys, pre, fs, _, fz, force, hz, sem):
+                f2[c, rows[k], :] = value
+
+            q1, q2 = vector(pre, rows[k], 12), vector(pre, rows[k], 18)
+            store_force(put, mixed(x[k], p2[k]), vector(ys, rows[k]), p1[k], q1, x[k], q2)
+        out_copy(f2, CX // 2, yb).start()
+    for first, src in ((0, fx), (CX // 2, f2)):
+        for yb in range(YB):
+            out_copy(src, first, yb).wait()
+
+
+def edge_z_kernel(far, near, ul, xs, ys, pre, fs, _, force, fz, hz, sem):
     def out_t(yb):
         return pltpu.make_async_copy(
             tiles(fs).at[pl.ds(18, 18), yb], force.at[3, :, :, :, lanes(yb)], sem.at[yb]
+        )
+
+    def out_z(yb):
+        return pltpu.make_async_copy(
+            tiles(fz).at[:, yb], force.at[2, :, :, :, lanes(yb)], sem.at[YB + yb]
         )
 
     for yb in range(YB):
@@ -399,8 +455,10 @@
 
     for yb in range(YB):
         lax.fori_loop(0, 4, body, yb)
+        out_z(yb).start()
     for yb in range(YB):
         out_t(yb).wait()
+        out_z(yb).wait()
 
 
 HBM = pl.BlockSpec(memory_space=pltpu.HBM)
@@ -446,60 +504,79 @@
         ),
         in_specs=[HBM] * 3,
         out_specs=[VM] * 6,
-        scratch_shapes=[dma((12,))],
+        scratch_shapes=[dma((15,))],
     )(links, solution, product)
     size = lax.axis_size("zt")
     near = lax.ppermute(near, "zt", [(i, i ^ 1) for i in range(size)])
-    far, xf, xb, ul, fs, pre = kernel_call(
+    far, ux, xf, xb, *work = kernel_call(
         early_kernel,
         "early",
         1000000,
         out_shape=(
             held(18, YB * CX, 128),
+            held(18, ROWS, 128),
             held(18, YB, CZ, 128),
             held(12, YB, CZ, 128),
             held(36, ROWS, 128),
             held(36, ROWS, 128),
-            held(24, ROWS, 128),
+            held(36, ROWS, 128),
+            held(18, ROWS, 128),
         ),
         in_specs=[HBM] + [VM] * 5,
-        out_specs=[VM] * 6,
-        input_output_aliases={5: 0},
-        scratch_shapes=[dma((6,))],
-    )(links, ux, uz, xs, ys, far)
+        out_specs=[VM] * 8,
+        input_output_aliases={4: 0, 5: 1},
+        scratch_shapes=[dma((9,))],
+    )(links, uz, xs, ys, far, ux)
     far = lax.ppermute(far, "zt", [(i, (i + 2 * (i % 2) - 1) % size) for i in range(size)])
     xb = shifted(xb, "xy", 1)
     xf = shifted(xf, "xy", -1)
-    _, fs, pre, force = kernel_call(
+    ux, _, fs, pre, fx, force = kernel_call(
         local_kernel,
         "local",
         LOCAL_COST,
-        out_shape=(held(36, ROWS, 128), held(36, ROWS, 128), held(24, ROWS, 128), FORCE),
-        in_specs=[HBM] + [VM] * 7,
-        out_specs=[VM, VM, VM, HBM],
-        input_output_aliases={5: 0, 6: 1, 7: 2},
-        scratch_shapes=[dma((6,)), dma((12,))],
-    )(links, ux, uz, xs, ys, ul, fs, pre)
-    fz, force = kernel_call(
+        out_shape=(
+            held(18, ROWS, 128),
+            held(36, ROWS, 128),
+            held(36, ROWS, 128),
+            held(36, ROWS, 128),
+            held(18, ROWS, 128),
+            FORCE,
+        ),
+        in_specs=[HBM] + [VM] * 8,
+        out_specs=[VM] * 5 + [HBM],
+        input_output_aliases={4: 0, 5: 1, 6: 2, 7: 3, 8: 4},
+        scratch_shapes=[dma((9,)), dma((12,))],
+    )(links, uz, xs, ys, ux, *work)
+    force = kernel_call(
         edge_z_kernel,
         "edge_z",
         EDGE_Z_COST,
-        out_shape=(held(18, ROWS, 128), FORCE),
-        in_specs=[VM] * 7 + [HBM],
-        out_specs=[VM, HBM],
-        input_output_aliases={7: 1},
-        scratch_shapes=[held(24, ROWS, 128), dma((3,))],
-    )(far, near, uz, xs, ys, pre, fs, force)
-    return kernel_call(
-        edge_x_kernel,
-        "edge_x",
-        4000000,
         out_shape=FORCE,
         in_specs=[VM] * 7 + [HBM],
         out_specs=HBM,
         input_output_aliases={7: 0},
+        scratch_shapes=[held(18, ROWS, 128), held(24, ROWS, 128), dma((6,))],
+    )(far, near, uz, xs, ys, pre, fs, force)
+    fx, force = kernel_call(
+        edge_back_kernel,
+        "edge_back",
+        4000000,
+        out_shape=(held(18, ROWS, 128), FORCE),
+        in_specs=[VM] * 5 + [HBM],
+        out_specs=[VM, HBM],
+        input_output_aliases={4: 0, 5: 1},
+        scratch_shapes=[held(12, YB * 8, 128)],
+    )(xb, ux, ys, pre, fx, force)
+    return kernel_call(
+        edge_ahead_kernel,
+        "edge_ahead",
+        4000000,
+        out_shape=FORCE,
+        in_specs=[VM] * 6 + [HBM],
+        out_specs=HBM,
+        input_output_aliases={6: 0},
         scratch_shapes=[held(18, ROWS, 128), held(18, YB * 8, 128), dma((6,))],
-    )(xf, xb, ux, xs, ys, pre, fz, force)
+    )(xf, ux, xs, ys, pre, fx, force)
 
 
 def solution(mesh):

time: 19.4 us -> 18.8 us (0.969)
  waiting for transfers between devices: 3.85 us -> 2.58 us
  starting transfers between devices: 5.48 us -> 6.2 us
    ppermute x1, waiting for transfers between devices: 2.7 us -> 1.6 us  [per_device(): lax.ppermute(far, 'zt', [(i, (i + 2 * (i % 2) - 1) % size) for i in range...]
    pallas_call x3 -> x4, Pallas kernels: 3.6 us -> 4.36 us  [the longest x1 1.73 us: per_device(): kernel_call(edge_z_kernel, 'edge_z', EDGE_Z_COST, out_shape=FORCE, in_spe...]
    ppermute x1, starting transfers between devices: 3.37 us -> 4.08 us  [per_device(): lax.ppermute(far, 'zt', [(i, (i + 2 * (i % 2) - 1) % size) for i in range...]
    pallas_call x1, Pallas kernels: 4.41 us -> 3.72 us  [per_device(): kernel_call(early_kernel, 'early', 1000000, out_shape=(held(18, YB * CX,...]
  transfers between devices with their start and end apart: 4 -> 4, of which waited for: 2 -> 2; matrix products, arithmetic and copies ran while one was open for 0% -> 0% of each run, Pallas kernels for 34% -> 38%
where the time goes in v4:
time: 18.8 us; the launch traced here: 18.6 us
  Pallas kernels  9.74 us (52%)
  starting transfers between devices  6.2 us (33%)
  waiting for transfers between devices  2.58 us (14%)
    ppermute x1, starting transfers between devices, per_device(): lax.ppermute(far, 'zt', [(i, (i + 2 * (i % 2) - 1) % size) for i in range...  4.08 us
    pallas_call x1, Pallas kernels, per_device(): kernel_call(early_kernel, 'early', 1000000, out_shape=(held(18, YB * CX,...  3.72 us
    ppermute x2, starting transfers between devices, shifted(): lax.ppermute(value, axis, [(i, (i + step) % size) for i in range(size)])  2.03 us
    pallas_call x1, Pallas kernels, per_device(): kernel_call(edge_z_kernel, 'edge_z', EDGE_Z_COST, out_shape=FORCE, in_spe...  1.73 us
    pallas_call x1, Pallas kernels, per_device(): kernel_call(prep_kernel, 'prep', 3000000, out_shape=(held(18, YB * CX, 12...  1.65 us
    ppermute x1, waiting for transfers between devices, per_device(): lax.ppermute(far, 'zt', [(i, (i + 2 * (i % 2) - 1) % size) for i in range...  1.6 us
    pallas_call x1, Pallas kernels, per_device(): kernel_call(local_kernel, 'local', LOCAL_COST, out_shape=(held(18, ROWS,...  1.44 us
    pallas_call x1, Pallas kernels, per_device(): kernel_call(edge_ahead_kernel, 'edge_ahead', 4000000, out_shape=FORCE, in...  1.05 us
  transfers between devices with their start and end apart: 4, of which 2 were waited for; matrix products, arithmetic and copies ran while one was open for 0% of the time, Pallas kernels for 38%

profile of v4, /device:TPU:26, one launch (start us, length us, event | category | flops | bytes accessed | tf_op | source)
XLA Modules:
  0.0 18.6 jit_solution(9985640641253988682)
XLA Ops:
  0.0 1.7 %prep.1 = (f32[18,24,128]{2,1,0:T(8,128)S(1)}, f32[20,24,128]{2,1,0:T(8,128)S(1)}, f32[18,96,128]{2,1,0:T(8,128)S(1)}, f32[18,96,128]{2,1,0:T(8,128)S(1)}, f32[6...) custom-call(f32[4,18,8,4,384]{4,3,2,1,0:T(4,128)} %links.5, f32[6,8,4,384]{3,2,1,0:T(4,128)} %sol.1, f32[6,8,4,384]{3,2,1,0:T(4,128)} %prod.1), custom_call_target="tpu_custom_call" | custom-call | flops 3000000 | bytes 3000000 | tf_op jit(solution)/shard_map/prep/pallas_call | solution.py:493
  1.7 0.1 collective-permute-start.3
  1.8 3.7 %early.1 = (f32[18,24,128]{2,1,0:T(8,128)S(1)}, f32[18,96,128]{2,1,0:T(8,128)S(1)}, f32[18,3,4,128]{3,2,1,0:T(4,128)S(1)}, f32[12,3,4,128]{3,2,1,0:T(4,128)S(1)}...) custom-call(f32[4,18,8,4,384]{4,3,2,1,0:T(4,128)} %links.5, ...), custom_call_target="tpu_custom_call", output_to_operand_aliasing={{0}: (4, {}), {1}: (5, {})} | custom-call | flops 1000000 | bytes 1000000 | tf_op jit(solution)/shard_map/early/pallas_call | solution.py:511
  5.5 4.1 %collective-permute-start.2 = (f32[18,24,128]{2,1,0:T(8,128)S(1)}, f32[18,24,128]{2,1,0:T(8,128)S(1)}, u32[]{:S(2)}, u32[]{:S(2)}) collective-permute-start(f32[18,24,128]{2,1,0:T(8,128)S(1)} %get-tuple-element.41), channel_id=1, source_target_pairs={{0,31},{1,2},{2,1},{3,4},{4,3},{5,6},{6,5},{7,8},{8,7},{9,10},{10,... | collective-permute-start | bytes 663560 | tf_op jit(solution)/shard_map/ppermute | solution.py:530
  9.6 1.1 %collective-permute-start.1 = (f32[12,3,4,128]{3,2,1,0:T(4,128)S(1)}, f32[12,3,4,128]{3,2,1,0:T(4,128)S(1)}, u32[]{:S(2)}, u32[]{:S(2)}) collective-permute-start(f32[12,3,4,128]{3,2,1,0:T(4,128)S(1)} %get-tuple-element.39), channel_id=1, source_target_pairs={{0,32},{32,64},{64,96},{96,128},{128,160},{160,192},{192,224},{224... | collective-permute-start | bytes 221192 | tf_op jit(solution)/shard_map/ppermute | solution.py:485
  10.7 0.9 %collective-permute-start = (f32[18,3,4,128]{3,2,1,0:T(4,128)S(1)}, f32[18,3,4,128]{3,2,1,0:T(4,128)S(1)}, u32[]{:S(2)}, u32[]{:S(2)}) collective-permute-start(f32[18,3,4,128]{3,2,1,0:T(4,128)S(1)} %get-tuple-element.31), channel_id=1, source_target_pairs={{0,224},{32,0},{64,32},{96,64},{128,96},{160,128},{192,160},{224,1... | collective-permute-start | bytes 331784 | tf_op jit(solution)/shard_map/ppermute | solution.py:485
  11.6 1.4 %local.1 = (f32[18,96,128]{2,1,0:T(8,128)S(1)}, f32[36,96,128]{2,1,0:T(8,128)S(1)}, f32[36,96,128]{2,1,0:T(8,128)S(1)}, f32[36,96,128]{2,1,0:T(8,128)S(1)}, f32[...) custom-call(f32[4,18,8,4,384]{4,3,2,1,0:T(4,128)} %links.5, ...), custom_call_target="tpu_custom_call", output_to_operand_aliasing={{0}: (4, {}), {1}: (5, {}), {2}: (6, {}), {3}: (7, {}), {4}... | custom-call | flops 1200000000 | bytes 1200000000 | tf_op jit(solution)/shard_map/local/pallas_call | solution.py:533
  13.1 1.6 %collective-permute-done.2.far = f32[18,24,128]{2,1,0:T(8,128)S(1)} collective-permute-done((f32[18,24,128]{2,1,0:T(8,128)S(1)}, f32[18,24,128]{2,1,0:T(8,128)S(1)}, u32[]{:S(2)}, u32[]{:S(2)}) %collective-permute-start.2) | collective-permute-done | bytes 221216 | tf_op jit(solution)/shard_map/ppermute | solution.py:530
  14.7 0.0 collective-permute-done.3.near
  14.7 1.7 %edge_z.1.__ = f32[4,18,8,4,384]{4,3,2,1,0:T(4,128)} custom-call(f32[18,24,128]{2,1,0:T(8,128)S(1)} %collective-permute-done.2.far, f32[20,24,128]{2,1,0:T(8,128)S(1)} %collective-permute-done.3.near, f32[18,96,128]{2,1,0:T(8,128)S(1)} %get-tuple-element.26.uz.ul, f32[6,96,128]{2,1,0:T(8,128)S(1)} %get-tuple-element.27.xs, ...), custom_call_target="tpu_custom_call", output_to_operand_aliasing={{}: (7, {})} | custom-call | flops 4000000 | bytes 4000000 | tf_op jit(solution)/shard_map/edge_z/pallas_call | solution.py:550
  16.4 0.0 collective-permute-done.1.xb
  16.4 0.1 edge_back.1
  16.5 1.0 %collective-permute-done.xf = f32[18,3,4,128]{3,2,1,0:T(4,128)S(1)} collective-permute-done((f32[18,3,4,128]{3,2,1,0:T(4,128)S(1)}, f32[18,3,4,128]{3,2,1,0:T(4,128)S(1)}, u32[]{:S(2)}, u32[]{:S(2)}) %collective-permute-start) | collective-permute-done | bytes 110624 | tf_op jit(solution)/shard_map/ppermute | solution.py:485
  17.5 1.0 %edge_ahead.1 = f32[4,18,8,4,384]{4,3,2,1,0:T(4,128)} custom-call(f32[18,3,4,128]{3,2,1,0:T(4,128)S(1)} %collective-permute-done.xf, f32[18,96,128]{2,1,0:T(8,128)S(1)} %get-tuple-element.37.ux, f32[6,96,128]{2,1,0:T(8,128)S(1)} %get-tuple-element.27.xs, f32[6,96,128]{2,1,0:T(8,128)S(1)} %get-tuple-element.28.ys, ...), custom_call_target="tpu_custom_call", output_to_operand_aliasing={{}: (6, {})} | custom-call | flops 4000000 | bytes 4000000 | tf_op jit(solution)/shard_map/edge_ahead/pallas_call | solution.py:570
Async XLA Ops:
  1.7 13.0 %collective-permute-start.3 = (f32[20,24,128]{2,1,0:T(8,128)S(1)}, f32[20,24,128]{2,1,0:T(8,128)S(1)}, u32[]{:S(2)}, u32[]{:S(2)}) collective-permute-start(f32[20,24,128]{2,1,0:T(8,128)S(1)} %get-tuple-element.42), channel_id=1, source_target_pairs={{0,1},{1,0},{2,3},{3,2},{4,5},{5,4},{6,7},{7,6},{8,9},{9,8},{10,11... | collective-permute-start | bytes 737288 | tf_op jit(solution)/shard_map/ppermute | solution.py:510
  5.5 9.2 %collective-permute-start.2 = (f32[18,24,128]{2,1,0:T(8,128)S(1)}, f32[18,24,128]{2,1,0:T(8,128)S(1)}, u32[]{:S(2)}, u32[]{:S(2)}) collective-permute-start(f32[18,24,128]{2,1,0:T(8,128)S(1)} %get-tuple-element.41), channel_id=1, source_target_pairs={{0,31},{1,2},{2,1},{3,4},{4,3},{5,6},{6,5},{7,8},{8,7},{9,10},{10,... | collective-permute-start | bytes 663560 | tf_op jit(solution)/shard_map/ppermute | solution.py:530
  9.6 6.8 %collective-permute-start.1 = (f32[12,3,4,128]{3,2,1,0:T(4,128)S(1)}, f32[12,3,4,128]{3,2,1,0:T(4,128)S(1)}, u32[]{:S(2)}, u32[]{:S(2)}) collective-permute-start(f32[12,3,4,128]{3,2,1,0:T(4,128)S(1)} %get-tuple-element.39), channel_id=1, source_target_pairs={{0,32},{32,64},{64,96},{96,128},{128,160},{160,192},{192,224},{224... | collective-permute-start | bytes 221192 | tf_op jit(solution)/shard_map/ppermute | solution.py:485
  10.7 6.9 %collective-permute-start = (f32[18,3,4,128]{3,2,1,0:T(4,128)S(1)}, f32[18,3,4,128]{3,2,1,0:T(4,128)S(1)}, u32[]{:S(2)}, u32[]{:S(2)}) collective-permute-start(f32[18,3,4,128]{3,2,1,0:T(4,128)S(1)} %get-tuple-element.31), channel_id=1, source_target_pairs={{0,224},{32,0},{64,32},{96,64},{128,96},{160,128},{192,160},{224,1... | collective-permute-start | bytes 331784 | tf_op jit(solution)/shard_map/ppermute | solution.py:485

commit v5 on v4

--- a/solution.py
+++ b/solution.py
@@ -14,10 +14,11 @@
 
 F32 = jnp.float32
 
-LOCAL_COST = 1200000000
+LOCAL_COST = 1000000
 EDGE_Z_COST = 4000000
-
-AHEAD = (4, 1)
+EDGE_BACK_COST = 2000000000
+
+AHEAD = (2, 0)
 
 
 def mat_vec(u, v):
@@ -87,7 +88,7 @@
     return [ref[first + c, rows, :] for c in range(6)]
 
 
-def prep_kernel(links, sol, prod, far, near, ux, uz, xs, ys, sem):
+def prep_kernel(links, sol, prod, far, near, xf, xb, ux, uz, xs, ys, sem):
     loads = Loads(sem)
     uxt, uzt, xst, yst = tiles(ux), tiles(uz), tiles(xs), tiles(ys)
     for yb in range(YB):
@@ -127,6 +128,21 @@
     pl.when(odd == 0)(lambda: put(far, near))
     pl.when(odd == 1)(lambda: put(near, far))
     loads.wait("ux")
+
+    def u_x(row):
+        return lambda c: ux[c, pl.ds(row, 8), :]
+
+    for yb in range(YB):
+        last = yb * CX * CZ + (CX - 2) * CZ
+        w1 = [coef_naik * v for v in adj_vec(u_x(last), vector(ys, pl.ds(last, 8)))]
+        w2 = adj_vec(u_x(last), [pltpu.roll(v, 4, 0) for v in w1])
+        for c, value in enumerate(w1 + w2):
+            xb[c, yb] = value[CZ:]
+        base = yb * CX * CZ
+        p1 = mat_vec(u_x(base), vector(xs, pl.ds(base + CZ, 8)))
+        p2 = mat_vec(u_x(base), [pltpu.roll(v, 4, 0) for v in p1])
+        for c, value in enumerate(vector(xs, pl.ds(base, 8)) + p1 + p2):
+            xf[c, yb] = value[:CZ]
 
 
 def move_y(v, step):
@@ -275,22 +291,7 @@
     lax.fori_loop(0, YB, body_x, 0)
 
 
-def early_kernel(links, uz, xs, ys, _, __, far, ux, xf, xb, ul, fs, pre, fx, sem):
-    def u_x(row):
-        return lambda c: ux[c, pl.ds(row, 8), :]
-
-    for yb in range(YB):
-        last = yb * CX * CZ + (CX - 2) * CZ
-        w1 = [coef_naik * v for v in adj_vec(u_x(last), vector(ys, pl.ds(last, 8)))]
-        w2 = adj_vec(u_x(last), [pltpu.roll(v, 4, 0) for v in w1])
-        for c, value in enumerate(w1 + w2):
-            xb[c, yb] = value[CZ:]
-        base = yb * CX * CZ
-        p1 = mat_vec(u_x(base), vector(xs, pl.ds(base + CZ, 8)))
-        p2 = mat_vec(u_x(base), [pltpu.roll(v, 4, 0) for v in p1])
-        for c, value in enumerate(vector(xs, pl.ds(base, 8)) + p1 + p2):
-            xf[c, yb] = value[:CZ]
-
+def early_kernel(links, uz, xs, ys, _, __, far, ux, ul, fs, pre, fx, sem):
     @pl.when(lax.axis_index("zt") == 0)
     def _():
         loads = Loads(sem)
@@ -357,7 +358,10 @@
         store_force(put, v1, vector(ys, rows), p1, q1, x, q2)
 
 
-def edge_ahead_kernel(xf, ux, xs, ys, pre, fx, _, force, f2, hx, sem):
+def edge_ahead_kernel(xf, ux, xs, ys, pre, fx, fz, _, force, f2, hx, sem):
+    for yb in range(1, YB):
+        out_z(fz, force, yb, sem.at[2 * YB + yb - 1]).start()
+
     def out_copy(src, first, yb):
         return pltpu.make_async_copy(
             tiles(src).at[:, yb, pl.ds(first, CX // 2)],
@@ -394,17 +398,18 @@
     for first, src in ((0, fx), (CX // 2, f2)):
         for yb in range(YB):
             out_copy(src, first, yb).wait()
-
-
-def edge_z_kernel(far, near, ul, xs, ys, pre, fs, _, force, fz, hz, sem):
+    for yb in range(1, YB):
+        out_z(fz, force, yb, sem.at[2 * YB + yb - 1]).wait()
+
+
+def out_z(fz, force, yb, sem):
+    return pltpu.make_async_copy(tiles(fz).at[:, yb], force.at[2, :, :, :, lanes(yb)], sem)
+
+
+def edge_z_kernel(far, near, ul, xs, ys, pre, fs, _, fz, force, hz, sem):
     def out_t(yb):
         return pltpu.make_async_copy(
             tiles(fs).at[pl.ds(18, 18), yb], force.at[3, :, :, :, lanes(yb)], sem.at[yb]
-        )
-
-    def out_z(yb):
-        return pltpu.make_async_copy(
-            tiles(fz).at[:, yb], force.at[2, :, :, :, lanes(yb)], sem.at[YB + yb]
         )
 
     for yb in range(YB):
@@ -455,10 +460,11 @@
 
     for yb in range(YB):
         lax.fori_loop(0, 4, body, yb)
-        out_z(yb).start()
+        if yb == 0:
+            out_z(fz, force, yb, sem.at[YB]).start()
     for yb in range(YB):
         out_t(yb).wait()
-        out_z(yb).wait()
+    out_z(fz, force, 0, sem.at[YB]).wait()
 
 
 HBM = pl.BlockSpec(memory_space=pltpu.HBM)
@@ -490,40 +496,40 @@
         pltpu.with_memory_space_constraint(a, pltpu.HBM) for a in (links, solution, product)
     )
     dma = pltpu.SemaphoreType.DMA
-    far, near, ux, uz, xs, ys = kernel_call(
+    far, near, xf, xb, ux, uz, xs, ys = kernel_call(
         prep_kernel,
         "prep",
         3000000,
         out_shape=(
             held(18, YB * CX, 128),
             held(20, YB * CX, 128),
+            held(18, YB, CZ, 128),
+            held(12, YB, CZ, 128),
             held(18, ROWS, 128),
             held(18, ROWS, 128),
             held(6, ROWS, 128),
             held(6, ROWS, 128),
         ),
         in_specs=[HBM] * 3,
-        out_specs=[VM] * 6,
+        out_specs=[VM] * 8,
         scratch_shapes=[dma((15,))],
     )(links, solution, product)
     size = lax.axis_size("zt")
     near = lax.ppermute(near, "zt", [(i, i ^ 1) for i in range(size)])
-    far, ux, xf, xb, *work = kernel_call(
+    far, ux, *work = kernel_call(
         early_kernel,
         "early",
         1000000,
         out_shape=(
             held(18, YB * CX, 128),
             held(18, ROWS, 128),
-            held(18, YB, CZ, 128),
-            held(12, YB, CZ, 128),
             held(36, ROWS, 128),
             held(36, ROWS, 128),
             held(36, ROWS, 128),
             held(18, ROWS, 128),
         ),
         in_specs=[HBM] + [VM] * 5,
-        out_specs=[VM] * 8,
+        out_specs=[VM] * 6,
         input_output_aliases={4: 0, 5: 1},
         scratch_shapes=[dma((9,))],
     )(links, uz, xs, ys, far, ux)
@@ -547,36 +553,36 @@
         input_output_aliases={4: 0, 5: 1, 6: 2, 7: 3, 8: 4},
         scratch_shapes=[dma((9,)), dma((12,))],
     )(links, uz, xs, ys, ux, *work)
-    force = kernel_call(
-        edge_z_kernel,
-        "edge_z",
-        EDGE_Z_COST,
-        out_shape=FORCE,
-        in_specs=[VM] * 7 + [HBM],
-        out_specs=HBM,
-        input_output_aliases={7: 0},
-        scratch_shapes=[held(18, ROWS, 128), held(24, ROWS, 128), dma((6,))],
-    )(far, near, uz, xs, ys, pre, fs, force)
     fx, force = kernel_call(
         edge_back_kernel,
         "edge_back",
-        4000000,
+        EDGE_BACK_COST,
         out_shape=(held(18, ROWS, 128), FORCE),
         in_specs=[VM] * 5 + [HBM],
         out_specs=[VM, HBM],
         input_output_aliases={4: 0, 5: 1},
         scratch_shapes=[held(12, YB * 8, 128)],
     )(xb, ux, ys, pre, fx, force)
+    fz, force = kernel_call(
+        edge_z_kernel,
+        "edge_z",
+        EDGE_Z_COST,
+        out_shape=(held(18, ROWS, 128), FORCE),
+        in_specs=[VM] * 7 + [HBM],
+        out_specs=[VM, HBM],
+        input_output_aliases={7: 1},
+        scratch_shapes=[held(24, ROWS, 128), dma((4,))],
+    )(far, near, uz, xs, ys, pre, fs, force)
     return kernel_call(
         edge_ahead_kernel,
         "edge_ahead",
         4000000,
         out_shape=FORCE,
-        in_specs=[VM] * 6 + [HBM],
+        in_specs=[VM] * 7 + [HBM],
         out_specs=HBM,
-        input_output_aliases={6: 0},
-        scratch_shapes=[held(18, ROWS, 128), held(18, YB * 8, 128), dma((6,))],
-    )(xf, ux, xs, ys, pre, fx, force)
+        input_output_aliases={7: 0},
+        scratch_shapes=[held(18, ROWS, 128), held(18, YB * 8, 128), dma((8,))],
+    )(xf, ux, xs, ys, pre, fx, fz, force)
 
 
 def solution(mesh):

time: 18.8 us -> 18.4 us (0.979)
  starting transfers between devices: 6.2 us -> 7.96 us
  waiting for transfers between devices: 2.58 us -> 0.83 us
  Pallas kernels: 9.74 us -> 9.25 us
    ppermute x2, starting transfers between devices: 2.03 us -> 4.15 us  [shifted(): lax.ppermute(value, axis, [(i, (i + step) % size) for i in range(size)])]
    pallas_call x1, Pallas kernels: 3.72 us -> 2.45 us  [per_device(): kernel_call(early_kernel, 'early', 1000000, out_shape=(held(18, YB * CX,...]
    pallas_call x1, Pallas kernels: 1.44 us -> 2.58 us  [per_device(): kernel_call(local_kernel, 'local', LOCAL_COST, out_shape=(held(18, ROWS,...]
    ppermute x1, waiting for transfers between devices: 1.6 us -> 0.47 us  [per_device(): lax.ppermute(far, 'zt', [(i, (i + 2 * (i % 2) - 1) % size) for i in range...]
    ppermute x2, waiting for transfers between devices: 0.99 us -> 0.35 us  [shifted(): lax.ppermute(value, axis, [(i, (i + step) % size) for i in range(size)])]
    pallas_call x2, Pallas kernels: 1.87 us -> 1.27 us  [the longest x1 1.13 us: per_device(): kernel_call(edge_z_kernel, 'edge_z', EDGE_Z_COST, out_shape=(held(18, ROW...]
    ppermute x1, starting transfers between devices: 4.08 us -> 3.8 us  [per_device(): lax.ppermute(far, 'zt', [(i, (i + 2 * (i % 2) - 1) % size) for i in range...]
  transfers between devices with their start and end apart: 4 -> 4, of which waited for: 2 -> 2; matrix products, arithmetic and copies ran while one was open for 0% -> 0% of each run, Pallas kernels for 38% -> 35%
where the time goes in v5:
time: 18.4 us; the launch traced here: 18.1 us
  Pallas kernels  9.25 us (50%)
  starting transfers between devices  7.96 us (43%)
  waiting for transfers between devices  0.83 us (5%)
    ppermute x2, starting transfers between devices, shifted(): lax.ppermute(value, axis, [(i, (i + step) % size) for i in range(size)])  4.15 us
    ppermute x1, starting transfers between devices, per_device(): lax.ppermute(far, 'zt', [(i, (i + 2 * (i % 2) - 1) % size) for i in range...  3.8 us
    pallas_call x1, Pallas kernels, per_device(): kernel_call(local_kernel, 'local', LOCAL_COST, out_shape=(held(18, ROWS,...  2.58 us
    pallas_call x1, Pallas kernels, per_device(): kernel_call(early_kernel, 'early', 1000000, out_shape=(held(18, YB * CX,...  2.45 us
    pallas_call x1, Pallas kernels, per_device(): kernel_call(prep_kernel, 'prep', 3000000, out_shape=(held(18, YB * CX, 12...  1.78 us
    pallas_call x1, Pallas kernels, per_device(): kernel_call(edge_ahead_kernel, 'edge_ahead', 4000000, out_shape=FORCE, in...  1.17 us
    pallas_call x1, Pallas kernels, per_device(): kernel_call(edge_z_kernel, 'edge_z', EDGE_Z_COST, out_shape=(held(18, ROW...  1.13 us
    ppermute x1, waiting for transfers between devices, per_device(): lax.ppermute(far, 'zt', [(i, (i + 2 * (i % 2) - 1) % size) for i in range...  0.47 us
  transfers between devices with their start and end apart: 4, of which 2 were waited for; matrix products, arithmetic and copies ran while one was open for 0% of the time, Pallas kernels for 35%

profile of v5, /device:TPU:26, one launch (start us, length us, event | category | flops | bytes accessed | tf_op | source)
XLA Modules:
  0.0 18.1 jit_solution(6246630884851959784)
XLA Ops:
  0.0 1.8 %prep.1 = (f32[18,24,128]{2,1,0:T(8,128)S(1)}, f32[20,24,128]{2,1,0:T(8,128)S(1)}, f32[18,3,4,128]{3,2,1,0:T(4,128)S(1)}, f32[12,3,4,128]{3,2,1,0:T(4,128)S(1)},...) custom-call(f32[4,18,8,4,384]{4,3,2,1,0:T(4,128)} %links.5, ...), custom_call_target="tpu_custom_call" | custom-call | flops 3000000 | bytes 3000000 | tf_op jit(solution)/shard_map/prep/pallas_call | solution.py:499
  1.8 2.0 %collective-permute-start.1 = (f32[12,3,4,128]{3,2,1,0:T(4,128)S(1)}, f32[12,3,4,128]{3,2,1,0:T(4,128)S(1)}, u32[]{:S(2)}, u32[]{:S(2)}) collective-permute-start(f32[12,3,4,128]{3,2,1,0:T(4,128)S(1)} %get-tuple-element.41), channel_id=1, source_target_pairs={{0,32},{32,64},{64,96},{96,128},{128,160},{160,192},{192,224},{224... | collective-permute-start | bytes 221192 | tf_op jit(solution)/shard_map/ppermute | solution.py:491
  3.8 0.0 collective-permute-start.3
  3.8 2.4 %early.1 = (f32[18,24,128]{2,1,0:T(8,128)S(1)}, f32[18,96,128]{2,1,0:T(8,128)S(1)}, f32[36,96,128]{2,1,0:T(8,128)S(1)}, f32[36,96,128]{2,1,0:T(8,128)S(1)}, f32[...) custom-call(f32[4,18,8,4,384]{4,3,2,1,0:T(4,128)} %links.5, ...), custom_call_target="tpu_custom_call", output_to_operand_aliasing={{0}: (4, {}), {1}: (5, {})} | custom-call | flops 1000000 | bytes 1000000 | tf_op jit(solution)/shard_map/early/pallas_call | solution.py:519
  6.3 3.8 %collective-permute-start.2 = (f32[18,24,128]{2,1,0:T(8,128)S(1)}, f32[18,24,128]{2,1,0:T(8,128)S(1)}, u32[]{:S(2)}, u32[]{:S(2)}) collective-permute-start(f32[18,24,128]{2,1,0:T(8,128)S(1)} %get-tuple-element.45), channel_id=1, source_target_pairs={{0,31},{1,2},{2,1},{3,4},{4,3},{5,6},{6,5},{7,8},{8,7},{9,10},{10,... | collective-permute-start | bytes 663560 | tf_op jit(solution)/shard_map/ppermute | solution.py:536
  10.1 2.1 %collective-permute-start = (f32[18,3,4,128]{3,2,1,0:T(4,128)S(1)}, f32[18,3,4,128]{3,2,1,0:T(4,128)S(1)}, u32[]{:S(2)}, u32[]{:S(2)}) collective-permute-start(f32[18,3,4,128]{3,2,1,0:T(4,128)S(1)} %get-tuple-element.28), channel_id=1, source_target_pairs={{0,224},{32,0},{64,32},{96,64},{128,96},{160,128},{192,160},{224,1... | collective-permute-start | bytes 331784 | tf_op jit(solution)/shard_map/ppermute | solution.py:491
  12.2 2.6 %local.1 = (f32[18,96,128]{2,1,0:T(8,128)S(1)}, f32[36,96,128]{2,1,0:T(8,128)S(1)}, f32[36,96,128]{2,1,0:T(8,128)S(1)}, f32[36,96,128]{2,1,0:T(8,128)S(1)}, f32[...) custom-call(f32[4,18,8,4,384]{4,3,2,1,0:T(4,128)} %links.5, ...), custom_call_target="tpu_custom_call", output_to_operand_aliasing={{0}: (4, {}), {1}: (5, {}), {2}: (6, {}), {3}: (7, {}), {4}... | custom-call | flops 1000000 | bytes 1000000 | tf_op jit(solution)/shard_map/local/pallas_call | solution.py:539
  14.8 0.0 collective-permute-done.1.xb
  14.8 0.1 edge_back.1
  14.9 0.5 %collective-permute-done.2.far = f32[18,24,128]{2,1,0:T(8,128)S(1)} collective-permute-done((f32[18,24,128]{2,1,0:T(8,128)S(1)}, f32[18,24,128]{2,1,0:T(8,128)S(1)}, u32[]{:S(2)}, u32[]{:S(2)}) %collective-permute-start.2) | collective-permute-done | bytes 221216 | tf_op jit(solution)/shard_map/ppermute | solution.py:536
  15.4 0.0 collective-permute-done.3.near
  15.4 1.1 %edge_z.1 = (f32[18,96,128]{2,1,0:T(8,128)S(1)}, f32[4,18,8,4,384]{4,3,2,1,0:T(4,128)}) custom-call(f32[18,24,128]{2,1,0:T(8,128)S(1)} %collective-permute-done.2.far, f32[20,24,128]{2,1,0:T(8,128)S(1)} %collective-permute-done.3.near, f32[18,96,128]{2,1,0:T(8,128)S(1)} %get-tuple-element.29.uz.ul, ...), custom_call_target="tpu_custom_call", output_to_operand_aliasing={{1}: (7, {})} | custom-call | flops 4000000 | bytes 4000000 | tf_op jit(solution)/shard_map/edge_z/pallas_call | solution.py:566
  16.6 0.4 %collective-permute-done.xf = f32[18,3,4,128]{3,2,1,0:T(4,128)S(1)} collective-permute-done((f32[18,3,4,128]{3,2,1,0:T(4,128)S(1)}, f32[18,3,4,128]{3,2,1,0:T(4,128)S(1)}, u32[]{:S(2)}, u32[]{:S(2)}) %collective-permute-start) | collective-permute-done | bytes 110624 | tf_op jit(solution)/shard_map/ppermute | solution.py:491
  16.9 1.2 %edge_ahead.1 = f32[4,18,8,4,384]{4,3,2,1,0:T(4,128)} custom-call(f32[18,3,4,128]{3,2,1,0:T(4,128)S(1)} %collective-permute-done.xf, f32[18,96,128]{2,1,0:T(8,128)S(1)} %get-tuple-element.39.ux, f32[6,96,128]{2,1,0:T(8,128)S(1)} %get-tuple-element.30.xs, f32[6,96,128]{2,1,0:T(8,128)S(1)} %get-tuple-element.31.ys, ...), custom_call_target="tpu_custom_call", output_to_operand_aliasing={{}: (7, {})} | custom-call | flops 4000000 | bytes 4000000 | tf_op jit(solution)/shard_map/edge_ahead/pallas_call | solution.py:576
Async XLA Ops:
  1.8 13.0 %collective-permute-start.1 = (f32[12,3,4,128]{3,2,1,0:T(4,128)S(1)}, f32[12,3,4,128]{3,2,1,0:T(4,128)S(1)}, u32[]{:S(2)}, u32[]{:S(2)}) collective-permute-start(f32[12,3,4,128]{3,2,1,0:T(4,128)S(1)} %get-tuple-element.41), channel_id=1, source_target_pairs={{0,32},{32,64},{64,96},{96,128},{128,160},{160,192},{192,224},{224... | collective-permute-start | bytes 221192 | tf_op jit(solution)/shard_map/ppermute | solution.py:491
  3.8 11.6 %collective-permute-start.3 = (f32[20,24,128]{2,1,0:T(8,128)S(1)}, f32[20,24,128]{2,1,0:T(8,128)S(1)}, u32[]{:S(2)}, u32[]{:S(2)}) collective-permute-start(f32[20,24,128]{2,1,0:T(8,128)S(1)} %get-tuple-element.46), channel_id=1, source_target_pairs={{0,1},{1,0},{2,3},{3,2},{4,5},{5,4},{6,7},{7,6},{8,9},{9,8},{10,11... | collective-permute-start | bytes 737288 | tf_op jit(solution)/shard_map/ppermute | solution.py:518
  6.3 9.2 %collective-permute-start.2 = (f32[18,24,128]{2,1,0:T(8,128)S(1)}, f32[18,24,128]{2,1,0:T(8,128)S(1)}, u32[]{:S(2)}, u32[]{:S(2)}) collective-permute-start(f32[18,24,128]{2,1,0:T(8,128)S(1)} %get-tuple-element.45), channel_id=1, source_target_pairs={{0,31},{1,2},{2,1},{3,4},{4,3},{5,6},{6,5},{7,8},{8,7},{9,10},{10,... | collective-permute-start | bytes 663560 | tf_op jit(solution)/shard_map/ppermute | solution.py:536
  10.1 6.9 %collective-permute-start = (f32[18,3,4,128]{3,2,1,0:T(4,128)S(1)}, f32[18,3,4,128]{3,2,1,0:T(4,128)S(1)}, u32[]{:S(2)}, u32[]{:S(2)}) collective-permute-start(f32[18,3,4,128]{3,2,1,0:T(4,128)S(1)} %get-tuple-element.28), channel_id=1, source_target_pairs={{0,224},{32,0},{64,32},{96,64},{128,96},{160,128},{192,160},{224,1... | collective-permute-start | bytes 331784 | tf_op jit(solution)/shard_map/ppermute | solution.py:491

commit v6 on v5

--- a/solution.py
+++ b/solution.py
@@ -502,7 +502,7 @@
         3000000,
         out_shape=(
             held(18, YB * CX, 128),
-            held(20, YB * CX, 128),
+            held(28, YB * CX, 128),
             held(18, YB, CZ, 128),
             held(12, YB, CZ, 128),
             held(18, ROWS, 128),

time: 18.4 us -> 18.1 us (0.984)
  starting transfers between devices: 7.96 us -> 7.69 us
    ppermute x1, starting transfers between devices: 3.8 us -> 3.45 us  [per_device(): lax.ppermute(far, 'zt', [(i, (i + 2 * (i % 2) - 1) % size) for i in range...]
    ppermute x1, waiting for transfers between devices: 0.47 us -> 0.82 us  [per_device(): lax.ppermute(far, 'zt', [(i, (i + 2 * (i % 2) - 1) % size) for i in range...]
    ppermute x2, waiting for transfers between devices: 0.35 us -> 0.01 us  [shifted(): lax.ppermute(value, axis, [(i, (i + step) % size) for i in range(size)])]
  transfers between devices with their start and end apart: 4 -> 4, of which waited for: 2 -> 1; matrix products, arithmetic and copies ran while one was open for 0% -> 0% of each run, Pallas kernels for 35% -> 35%
where the time goes in v6:
time: 18.1 us; the launch traced here: 17.8 us
  Pallas kernels  9.26 us (51%)
  starting transfers between devices  7.69 us (42%)
  waiting for transfers between devices  0.83 us (5%)
    ppermute x2, starting transfers between devices, shifted(): lax.ppermute(value, axis, [(i, (i + step) % size) for i in range(size)])  4.15 us
    ppermute x1, starting transfers between devices, per_device(): lax.ppermute(far, 'zt', [(i, (i + 2 * (i % 2) - 1) % size) for i in range...  3.45 us
    pallas_call x1, Pallas kernels, per_device(): kernel_call(local_kernel, 'local', LOCAL_COST, out_shape=(held(18, ROWS,...  2.58 us
    pallas_call x1, Pallas kernels, per_device(): kernel_call(early_kernel, 'early', 1000000, out_shape=(held(18, YB * CX,...  2.45 us
    pallas_call x1, Pallas kernels, per_device(): kernel_call(prep_kernel, 'prep', 3000000, out_shape=(held(18, YB * CX, 12...  1.78 us
    pallas_call x1, Pallas kernels, per_device(): kernel_call(edge_ahead_kernel, 'edge_ahead', 4000000, out_shape=FORCE, in...  1.18 us
    pallas_call x1, Pallas kernels, per_device(): kernel_call(edge_z_kernel, 'edge_z', EDGE_Z_COST, out_shape=(held(18, ROW...  1.13 us
    ppermute x1, waiting for transfers between devices, per_device(): lax.ppermute(far, 'zt', [(i, (i + 2 * (i % 2) - 1) % size) for i in range...  0.82 us
  transfers between devices with their start and end apart: 4, of which 1 were waited for; matrix products, arithmetic and copies ran while one was open for 0% of the time, Pallas kernels for 35%

profile of v6, /device:TPU:26, one launch (start us, length us, event | category | flops | bytes accessed | tf_op | source)
XLA Modules:
  0.0 17.8 jit_solution(14551763175410436243)
XLA Ops:
  0.0 1.8 %prep.1 = (f32[18,24,128]{2,1,0:T(8,128)S(1)}, f32[28,24,128]{2,1,0:T(8,128)S(1)}, f32[18,3,4,128]{3,2,1,0:T(4,128)S(1)}, f32[12,3,4,128]{3,2,1,0:T(4,128)S(1)},...) custom-call(f32[4,18,8,4,384]{4,3,2,1,0:T(4,128)} %links.5, ...), custom_call_target="tpu_custom_call" | custom-call | flops 3000000 | bytes 3000000 | tf_op jit(solution)/shard_map/prep/pallas_call | solution.py:499
  1.8 0.1 collective-permute-start.3
  1.9 2.0 %collective-permute-start.1 = (f32[12,3,4,128]{3,2,1,0:T(4,128)S(1)}, f32[12,3,4,128]{3,2,1,0:T(4,128)S(1)}, u32[]{:S(2)}, u32[]{:S(2)}) collective-permute-start(f32[12,3,4,128]{3,2,1,0:T(4,128)S(1)} %get-tuple-element.41), channel_id=1, source_target_pairs={{0,32},{32,64},{64,96},{96,128},{128,160},{160,192},{192,224},{224... | collective-permute-start | bytes 221192 | tf_op jit(solution)/shard_map/ppermute | solution.py:491
  3.9 2.4 %early.1 = (f32[18,24,128]{2,1,0:T(8,128)S(1)}, f32[18,96,128]{2,1,0:T(8,128)S(1)}, f32[36,96,128]{2,1,0:T(8,128)S(1)}, f32[36,96,128]{2,1,0:T(8,128)S(1)}, f32[...) custom-call(f32[4,18,8,4,384]{4,3,2,1,0:T(4,128)} %links.5, ...), custom_call_target="tpu_custom_call", output_to_operand_aliasing={{0}: (4, {}), {1}: (5, {})} | custom-call | flops 1000000 | bytes 1000000 | tf_op jit(solution)/shard_map/early/pallas_call | solution.py:519
  6.3 3.5 %collective-permute-start.2 = (f32[18,24,128]{2,1,0:T(8,128)S(1)}, f32[18,24,128]{2,1,0:T(8,128)S(1)}, u32[]{:S(2)}, u32[]{:S(2)}) collective-permute-start(f32[18,24,128]{2,1,0:T(8,128)S(1)} %get-tuple-element.45), channel_id=1, source_target_pairs={{0,31},{1,2},{2,1},{3,4},{4,3},{5,6},{6,5},{7,8},{8,7},{9,10},{10,... | collective-permute-start | bytes 663560 | tf_op jit(solution)/shard_map/ppermute | solution.py:536
  9.8 2.1 %collective-permute-start = (f32[18,3,4,128]{3,2,1,0:T(4,128)S(1)}, f32[18,3,4,128]{3,2,1,0:T(4,128)S(1)}, u32[]{:S(2)}, u32[]{:S(2)}) collective-permute-start(f32[18,3,4,128]{3,2,1,0:T(4,128)S(1)} %get-tuple-element.28), channel_id=1, source_target_pairs={{0,224},{32,0},{64,32},{96,64},{128,96},{160,128},{192,160},{224,1... | collective-permute-start | bytes 331784 | tf_op jit(solution)/shard_map/ppermute | solution.py:491
  11.9 2.6 %local.1 = (f32[18,96,128]{2,1,0:T(8,128)S(1)}, f32[36,96,128]{2,1,0:T(8,128)S(1)}, f32[36,96,128]{2,1,0:T(8,128)S(1)}, f32[36,96,128]{2,1,0:T(8,128)S(1)}, f32[...) custom-call(f32[4,18,8,4,384]{4,3,2,1,0:T(4,128)} %links.5, ...), custom_call_target="tpu_custom_call", output_to_operand_aliasing={{0}: (4, {}), {1}: (5, {}), {2}: (6, {}), {3}: (7, {}), {4}... | custom-call | flops 1000000 | bytes 1000000 | tf_op jit(solution)/shard_map/local/pallas_call | solution.py:539
  14.5 0.0 collective-permute-done.1.xb
  14.5 0.1 edge_back.1
  14.7 0.8 %collective-permute-done.2.far = f32[18,24,128]{2,1,0:T(8,128)S(1)} collective-permute-done((f32[18,24,128]{2,1,0:T(8,128)S(1)}, f32[18,24,128]{2,1,0:T(8,128)S(1)}, u32[]{:S(2)}, u32[]{:S(2)}) %collective-permute-start.2) | collective-permute-done | bytes 221216 | tf_op jit(solution)/shard_map/ppermute | solution.py:536
  15.5 0.0 collective-permute-done.3.near
  15.5 1.1 %edge_z.1 = (f32[18,96,128]{2,1,0:T(8,128)S(1)}, f32[4,18,8,4,384]{4,3,2,1,0:T(4,128)}) custom-call(f32[18,24,128]{2,1,0:T(8,128)S(1)} %collective-permute-done.2.far, f32[28,24,128]{2,1,0:T(8,128)S(1)} %collective-permute-done.3.near, f32[18,96,128]{2,1,0:T(8,128)S(1)} %get-tuple-element.29.uz.ul, ...), custom_call_target="tpu_custom_call", output_to_operand_aliasing={{1}: (7, {})} | custom-call | flops 4000000 | bytes 4000000 | tf_op jit(solution)/shard_map/edge_z/pallas_call | solution.py:566
  16.7 0.0 collective-permute-done.xf
  16.7 1.2 %edge_ahead.1 = f32[4,18,8,4,384]{4,3,2,1,0:T(4,128)} custom-call(f32[18,3,4,128]{3,2,1,0:T(4,128)S(1)} %collective-permute-done.xf, f32[18,96,128]{2,1,0:T(8,128)S(1)} %get-tuple-element.39.ux, f32[6,96,128]{2,1,0:T(8,128)S(1)} %get-tuple-element.30.xs, f32[6,96,128]{2,1,0:T(8,128)S(1)} %get-tuple-element.31.ys, ...), custom_call_target="tpu_custom_call", output_to_operand_aliasing={{}: (7, {})} | custom-call | flops 4000000 | bytes 4000000 | tf_op jit(solution)/shard_map/edge_ahead/pallas_call | solution.py:576
Async XLA Ops:
  1.8 13.7 %collective-permute-start.3 = (f32[28,24,128]{2,1,0:T(8,128)S(1)}, f32[28,24,128]{2,1,0:T(8,128)S(1)}, u32[]{:S(2)}, u32[]{:S(2)}) collective-permute-start(f32[28,24,128]{2,1,0:T(8,128)S(1)} %get-tuple-element.46), channel_id=1, source_target_pairs={{0,1},{1,0},{2,3},{3,2},{4,5},{5,4},{6,7},{7,6},{8,9},{9,8},{10,11... | collective-permute-start | bytes 1032200 | tf_op jit(solution)/shard_map/ppermute | solution.py:518
  1.9 12.7 %collective-permute-start.1 = (f32[12,3,4,128]{3,2,1,0:T(4,128)S(1)}, f32[12,3,4,128]{3,2,1,0:T(4,128)S(1)}, u32[]{:S(2)}, u32[]{:S(2)}) collective-permute-start(f32[12,3,4,128]{3,2,1,0:T(4,128)S(1)} %get-tuple-element.41), channel_id=1, source_target_pairs={{0,32},{32,64},{64,96},{96,128},{128,160},{160,192},{192,224},{224... | collective-permute-start | bytes 221192 | tf_op jit(solution)/shard_map/ppermute | solution.py:491
  6.3 9.2 %collective-permute-start.2 = (f32[18,24,128]{2,1,0:T(8,128)S(1)}, f32[18,24,128]{2,1,0:T(8,128)S(1)}, u32[]{:S(2)}, u32[]{:S(2)}) collective-permute-start(f32[18,24,128]{2,1,0:T(8,128)S(1)} %get-tuple-element.45), channel_id=1, source_target_pairs={{0,31},{1,2},{2,1},{3,4},{4,3},{5,6},{6,5},{7,8},{8,7},{9,10},{10,... | collective-permute-start | bytes 663560 | tf_op jit(solution)/shard_map/ppermute | solution.py:536
  9.8 6.9 %collective-permute-start = (f32[18,3,4,128]{3,2,1,0:T(4,128)S(1)}, f32[18,3,4,128]{3,2,1,0:T(4,128)S(1)}, u32[]{:S(2)}, u32[]{:S(2)}) collective-permute-start(f32[18,3,4,128]{3,2,1,0:T(4,128)S(1)} %get-tuple-element.28), channel_id=1, source_target_pairs={{0,224},{32,0},{64,32},{96,64},{128,96},{160,128},{192,160},{224,1... | collective-permute-start | bytes 331784 | tf_op jit(solution)/shard_map/ppermute | solution.py:491
